TPU v7x, 32 devices: a whole 2x2x4 slice. The times are simulated.
32 devices in a mesh: dp: 16 (over z, y, core), seq: 2 (over x).
Axes of the slice: x: 2, y: 2, z: 4, core: 2. Of those that a mesh axis runs over, the one named last changes fastest.
Arguments:
- tokens: bfloat16 [32768, 768], P(('dp', 'seq')), may hold values from -8 to 8
- gain_attn: bfloat16 [768], P('dp'), may hold values from 0.25 to 1.75
- w_qkv: bfloat16 [768, 2304], P('dp'), may hold values from -0.3125 to 0.3125
- w_out: bfloat16 [768, 768], P('dp'), may hold values from -1.25 to 1.25
- gain_mlp: bfloat16 [768], P('dp'), may hold values from 0.25 to 1.75
- w_in: bfloat16 [768, 2304], P('dp'), may hold values from -0.21875 to 0.21875
- w_down: bfloat16 [1152, 768], P('dp'), may hold values from -0.1875 to 0.1875
- d_out: bfloat16 [32768, 768], P(('dp', 'seq')), may hold values from -6 to 6
Outputs:
- mixed: bfloat16 [32768, 768], P(('dp', 'seq'))
- grad_tokens: float32 [32768, 768], P(('dp', 'seq'))
- grad_gain_attn: float32 [768], P('dp')
- grad_w_qkv: float32 [768, 2304], P('dp')
- grad_w_out: float32 [768, 768], P('dp')
- grad_gain_mlp: float32 [768], P('dp')
- grad_w_in: float32 [768, 2304], P('dp')
- grad_w_down: float32 [1152, 768], P('dp')
All inputs are finite; a program needn't handle non-finite values.
Results may differ from a plain program's by a relative error of at most 0.017.
Values may be sent and summed in bfloat16 or wider, within the bound.
A program may use at most 256 MiB of HBM per device.

v0:
```python
import jax
import jax.numpy as jnp
from jax import lax
from jax.sharding import PartitionSpec as P

D = 768
HEADS = 12
HEAD_DIM = 64
FF = 1152


eps = 1e-05
rope_base = 160000.0


def normalize_rows(values_in, gain_vec):
    centre = values_in - jnp.mean(values_in, axis=-1, keepdims=True)
    spread = jnp.mean(centre * centre, axis=-1, keepdims=True)
    inv_std = lax.rsqrt(spread + eps)
    unit_rows = centre * inv_std
    return (unit_rows * gain_vec, unit_rows, inv_std)


def normalize_back(grad_normed, gain_vec, unit_rows, inv_std):
    grad_unit = grad_normed * gain_vec
    grad_in = inv_std * (
        grad_unit
        - jnp.mean(grad_unit, axis=-1, keepdims=True)
        - unit_rows * jnp.mean(grad_unit * unit_rows, axis=-1, keepdims=True)
    )
    return (grad_in, jnp.sum(grad_normed * unit_rows, axis=0))


def rotary_tables(positions):
    half_dim = HEAD_DIM // 2
    inverse = rope_base ** (-(jnp.arange(half_dim).astype(jnp.float32) * 2.0) / HEAD_DIM)
    phases = positions[:, None] * inverse[None, :]
    phases = jnp.concatenate([phases, phases], axis=-1)
    return (jnp.cos(phases), jnp.sin(phases))


def rotate(vectors, cos_table, sin_table):
    lower = vectors[..., : HEAD_DIM // 2]
    upper = vectors[..., HEAD_DIM // 2 :]
    turned = jnp.concatenate([-upper, lower], axis=-1)
    return vectors * cos_table[:, None, :] + turned * sin_table[:, None, :]


def gated(gate_part, up_part):
    return jax.nn.gelu(gate_part, approximate=False) * up_part


def body(tokens, gain_attn, w_qkv, w_out, gain_mlp, w_in, w_down, d_out):
    ways = lax.axis_size("seq")
    local_heads = HEADS // ways
    head_cols = local_heads * HEAD_DIM
    tok_rows = tokens.shape[0]
    seq_len = tok_rows * ways
    block_rows = min(512, seq_len)
    block_count = seq_len // block_rows
    score_scale = HEAD_DIM ** (-0.5)
    full = (
        lax.all_gather(gain_attn, "dp", axis=0, tiled=True),
        lax.all_gather(w_qkv, "dp", axis=0, tiled=True),
        lax.all_gather(w_out, "dp", axis=0, tiled=True),
        lax.all_gather(gain_mlp, "dp", axis=0, tiled=True),
        lax.all_gather(w_in, "dp", axis=0, tiled=True),
        lax.all_gather(w_down, "dp", axis=0, tiled=True),
    )
    inputs = tokens.astype(jnp.float32)
    normed_one, unit_one, inv_one = normalize_rows(inputs, full[0].astype(jnp.float32))
    act_one = normed_one.astype(jnp.bfloat16)
    projected = jnp.dot(act_one, full[1], preferred_element_type=jnp.float32).reshape(
        tok_rows, 3, HEADS, HEAD_DIM
    )
    positions = (lax.axis_index("seq") * tok_rows + jnp.arange(tok_rows)).astype(jnp.float32)
    cos_table, sin_table = rotary_tables(positions)
    rotated = jnp.stack(
        [
            rotate(projected[:, 0], cos_table, sin_table),
            rotate(projected[:, 1], cos_table, sin_table),
            projected[:, 2],
        ],
        axis=1,
    ).astype(jnp.bfloat16)
    arrived = lax.all_to_all(
        rotated.reshape(tok_rows, 3, ways, head_cols),
        "seq",
        split_axis=2,
        concat_axis=0,
        tiled=True,
    )
    head_view = arrived.reshape(seq_len, 3, local_heads, HEAD_DIM)
    queries = head_view[:, 0]
    key_rows = head_view[:, 1]
    value_rows = head_view[:, 2]
    q_blocks = queries.reshape(block_count, block_rows, local_heads, HEAD_DIM)

    def forward_block(q_block):
        scores = (
            jnp.einsum("qhd,khd->hqk", q_block, key_rows, preferred_element_type=jnp.float32)
            * score_scale
        )
        row_max = jnp.max(scores, axis=-1, keepdims=True)
        exp_scores = jnp.exp(scores - row_max)
        row_total = jnp.sum(exp_scores, axis=-1, keepdims=True)
        probs = (exp_scores / row_total).astype(jnp.bfloat16)
        out_block = jnp.einsum(
            "hqk,khd->qhd", probs, value_rows, preferred_element_type=jnp.float32
        )
        return (out_block.astype(jnp.bfloat16), (row_max + jnp.log(row_total))[..., 0])

    ctx_heads, log_sums = lax.map(forward_block, q_blocks)
    ctx_local = lax.all_to_all(
        ctx_heads.reshape(seq_len, 1, head_cols), "seq", split_axis=0, concat_axis=1, tiled=True
    ).reshape(tok_rows, D)
    attended = jnp.dot(ctx_local, full[2], preferred_element_type=jnp.float32)
    hidden = inputs + attended
    normed_two, unit_two, inv_two = normalize_rows(hidden, full[3].astype(jnp.float32))
    act_two = normed_two.astype(jnp.bfloat16)
    gate_up = jnp.dot(act_two, full[4], preferred_element_type=jnp.float32)
    gated_value, gated_pull = jax.vjp(gated, gate_up[:, :FF], gate_up[:, FF:])
    activated = gated_value.astype(jnp.bfloat16)
    mixed = (hidden + jnp.dot(activated, full[5], preferred_element_type=jnp.float32)).astype(
        jnp.bfloat16
    )
    back = (
        lax.all_gather(gain_attn, "dp", axis=0, tiled=True),
        lax.all_gather(w_qkv, "dp", axis=0, tiled=True),
        lax.all_gather(w_out, "dp", axis=0, tiled=True),
        lax.all_gather(gain_mlp, "dp", axis=0, tiled=True),
        lax.all_gather(w_in, "dp", axis=0, tiled=True),
        lax.all_gather(w_down, "dp", axis=0, tiled=True),
    )
    grad_out = d_out.astype(jnp.float32)
    grad_w_down = jnp.einsum("tf,td->fd", activated, d_out, preferred_element_type=jnp.float32)
    grad_act = jnp.einsum("td,fd->tf", d_out, back[5], preferred_element_type=jnp.float32)
    grad_gate, grad_up = gated_pull(grad_act)
    grad_gate_up = jnp.concatenate([grad_gate, grad_up], axis=1).astype(jnp.bfloat16)
    grad_w_in = jnp.einsum("td,tf->df", act_two, grad_gate_up, preferred_element_type=jnp.float32)
    grad_norm_two = jnp.einsum(
        "tf,df->td", grad_gate_up, back[4], preferred_element_type=jnp.float32
    )
    grad_hidden_norm, grad_gain_two = normalize_back(
        grad_norm_two, back[3].astype(jnp.float32), unit_two, inv_two
    )
    grad_hidden = grad_out + grad_hidden_norm
    grad_hidden_low = grad_hidden.astype(jnp.bfloat16)
    grad_w_out = jnp.einsum(
        "td,te->de", ctx_local, grad_hidden_low, preferred_element_type=jnp.float32
    )
    grad_ctx = jnp.einsum(
        "te,de->td", grad_hidden_low, back[2], preferred_element_type=jnp.float32
    ).astype(jnp.bfloat16)
    grad_ctx_heads = lax.all_to_all(
        grad_ctx.reshape(tok_rows, ways, head_cols), "seq", split_axis=1, concat_axis=0, tiled=True
    )
    grad_ctx_blocks = grad_ctx_heads.reshape(block_count, block_rows, local_heads, HEAD_DIM)

    def backward_block(carry, pieces):
        grad_keys, grad_values = carry
        q_block, g_block, lse_block = pieces
        scores = (
            jnp.einsum("qhd,khd->hqk", q_block, key_rows, preferred_element_type=jnp.float32)
            * score_scale
        )
        probs = jnp.exp(scores - lse_block[..., None])
        probs_low = probs.astype(jnp.bfloat16)
        grad_values = grad_values + jnp.einsum(
            "hqk,qhd->khd", probs_low, g_block, preferred_element_type=jnp.float32
        )
        grad_probs = jnp.einsum(
            "qhd,khd->hqk", g_block, value_rows, preferred_element_type=jnp.float32
        )
        row_dot = jnp.sum(probs * grad_probs, axis=-1, keepdims=True)
        grad_scores = (probs * (grad_probs - row_dot)).astype(jnp.bfloat16)
        grad_q = (
            jnp.einsum("hqk,khd->qhd", grad_scores, key_rows, preferred_element_type=jnp.float32)
            * score_scale
        )
        grad_keys = (
            grad_keys
            + jnp.einsum("hqk,qhd->khd", grad_scores, q_block, preferred_element_type=jnp.float32)
            * score_scale
        )
        return ((grad_keys, grad_values), grad_q)

    zero_heads = jnp.zeros((seq_len, local_heads, HEAD_DIM), jnp.float32)
    (grad_keys, grad_values), grad_queries = lax.scan(
        backward_block, (zero_heads, zero_heads), (q_blocks, grad_ctx_blocks, log_sums)
    )
    grad_queries = grad_queries.reshape(seq_len, local_heads, HEAD_DIM)
    cos_full, sin_full = rotary_tables(jnp.arange(seq_len).astype(jnp.float32))
    grad_heads = jnp.stack(
        [
            rotate(grad_queries, cos_full, -sin_full),
            rotate(grad_keys, cos_full, -sin_full),
            grad_values,
        ],
        axis=1,
    ).astype(jnp.bfloat16)
    grad_proj = lax.all_to_all(
        grad_heads.reshape(seq_len, 3, 1, head_cols), "seq", split_axis=0, concat_axis=2, tiled=True
    ).reshape(tok_rows, 3 * D)
    grad_w_qkv = jnp.einsum("td,te->de", act_one, grad_proj, preferred_element_type=jnp.float32)
    grad_norm_one = jnp.einsum("te,de->td", grad_proj, back[1], preferred_element_type=jnp.float32)
    grad_input_norm, grad_gain_one = normalize_back(
        grad_norm_one, back[0].astype(jnp.float32), unit_one, inv_one
    )
    grad_tokens = grad_hidden + grad_input_norm
    shards = (
        lax.psum_scatter(grad_gain_one, "dp", scatter_dimension=0, tiled=True),
        lax.psum_scatter(grad_w_qkv, "dp", scatter_dimension=0, tiled=True),
        lax.psum_scatter(grad_w_out, "dp", scatter_dimension=0, tiled=True),
        lax.psum_scatter(grad_gain_two, "dp", scatter_dimension=0, tiled=True),
        lax.psum_scatter(grad_w_in, "dp", scatter_dimension=0, tiled=True),
        lax.psum_scatter(grad_w_down, "dp", scatter_dimension=0, tiled=True),
    )
    summed = (
        lax.psum(shards[0].astype(jnp.bfloat16), "seq").astype(jnp.float32),
        lax.psum(shards[1].astype(jnp.bfloat16), "seq").astype(jnp.float32),
        lax.psum(shards[2].astype(jnp.bfloat16), "seq").astype(jnp.float32),
        lax.psum(shards[3].astype(jnp.bfloat16), "seq").astype(jnp.float32),
        lax.psum(shards[4].astype(jnp.bfloat16), "seq").astype(jnp.float32),
        lax.psum(shards[5].astype(jnp.bfloat16), "seq").astype(jnp.float32),
    )
    return (mixed, grad_tokens, summed[0], summed[1], summed[2], summed[3], summed[4], summed[5])


def solution(mesh):
    in_specs = (
        P(("dp", "seq"), None),
        P("dp"),
        P("dp", None),
        P("dp", None),
        P("dp"),
        P("dp", None),
        P("dp", None),
        P(("dp", "seq"), None),
    )
    out_specs = (
        P(("dp", "seq"), None),
        P(("dp", "seq"), None),
        P("dp"),
        P("dp", None),
        P("dp", None),
        P("dp"),
        P("dp", None),
        P("dp", None),
    )
    return jax.shard_map(body, mesh=mesh, in_specs=in_specs, out_specs=out_specs, check_vma=False)
```

profile of v0, /device:TPU:0, one launch (start us, length us, event | category | flops | bytes accessed | tf_op | source)
XLA Modules:
  0.0 1064.5 jit_solution(14553424392459026825)
XLA Ops:
  13.0 35.9 %all-reduce.5 = (bf16[768]{0:T(1024)(128)(2,1)S(1)}, bf16[768]{0:T(1024)(128)(2,1)}) all-reduce(bf16[768]{0:T(1024)(128)(2,1)S(1)} %dynamic-update-slice, bf16[768]{0:T(1024)(128)(2,1)S(1)} %dynamic-update-slice.1), channel_id=1, replica_groups=mesh['dp'=16,'seq'=2] {'dp'}, use_global_device_ids=true, to_apply=%add | all-reduce | flops 1536 | bytes 6144
  80.8 53.1 %all-to-all-done = bf16[1024,3,2,384]{0,3,1,2:T(8,128)(2,1)} async-done(((bf16[1024,3,2,384]{0,3,1,2:T(8,128)(2,1)}), bf16[1024,3,2,384]{0,3,1,2:T(8,128)(2,1)}, u32[]{:S(2)}, u32[]{:S(2)}) %all-to-all-start) | async-done | bytes 4718624 | tf_op jit(solution)/shard_map/all_to_all | solution.py:86
  159.5 104.2 %while.27 = (s32[]{:T(128)}, bf16[4,512,6,64]{1,3,2,0:T(8,128)(2,1)}, f32[4,6,512]{2,1,0:T(8,128)}, bf16[4,512,6,64]{1,3,2,0:T(8,128)(2,1)}, bf16[2048,6,64]{0,2...) while((s32[]{:T(128)}, bf16[4,512,6,64]{1,3,2,0:T(8,128)(2,1)}, f32[4,6,512]{2,1,0:T(8,128)}, ...), condition=%wide.region_5.6_spmd, body=%wide.region_2.5_spmd.sunk | while | flops 1667429376 | bytes 180196976 | solution.py:113
  319.3 16.1 %add_convert_fusion = (bf16[1024,1152]{1,0:T(8,128)(2,1)}, f32[1024,1152]{1,0:T(8,128)S(1)}, f32[1024,1152]{1,0:T(8,128)S(1)}) fusion(f32[1024,2304]{1,0:T(8,128)} %fusion.80, bf16[1024,768]{1,0:T(8,128)(2,1)S(1)} %copy-done.18, bf16[1152,768]{1,0:T(8,128)(2,1)} %all-gather.11.cloned.1.call-done), kind=kOutput, calls=%fused_computation.50 | convolution fusion | flops 1898053632 | bytes 24576000 | tf_op jit(solution)/shard_map/td,fd->tf/dot_general | solution.py:137
  401.6 404.0 %while.28 = (s32[]{:T(128)}, f32[2048,6,64]{0,2,1:T(8,128)}, f32[2048,6,64]{0,2,1:T(8,128)}, f32[4,512,6,64]{1,0,3,2:T(4,128)}, bf16[4,512,6,64]{1,3,2,0:T(8,128...) while((s32[]{:T(128)}, f32[2048,6,64]{0,2,1:T(8,128)}, ...), condition=%wide.region_12.13_spmd.clone, body=%wide.region_10.12_spmd.clone.sunk | while | flops 4106155008 | bytes 217929904 | solution.py:189
  413.7 16.9 %multiply_reduce_fusion.10 = (f32[6,512]{1,0:T(8,128)S(1)}, f32[6,512,2048]{2,1,0:T(8,128)}) fusion(f32[6,512,2048]{2,1,0:T(8,128)} %fusion.136, f32[6,512]{1,0:T(8,128)S(1)} %dynamic-slice_bitcast_fusion.2, bf16[2048,6,64]{0,2,1:T(8,128)(2,1)S(1)} %get-tuple-element.481, bf16[4,512,6,64]{1,3,2,0:T(8,128)(2,1)} %get-tuple-element.480, ...), kind=kOutput, calls=%fused_computation.15.clone.1 | convolution fusion | flops 830469120 | bytes 52322816 | tf_op jit(solution)/shard_map/while/body/eval_jaxpr/qhd,khd->hqk/dot_general | solution.py:172
  430.6 22.6 %multiply_convert_fusion.7 = bf16[6,512,2048]{2,1,0:T(8,128)(2,1)} fusion(f32[6,512,2048]{2,1,0:T(8,128)} %get-tuple-element.428, f32[6,512,2048]{2,1,0:T(8,128)} %fusion.136, f32[6,512]{1,0:T(8,128)S(1)} %get-tuple-element.429, f32[6,512]{1,0:T(8,128)S(1)} %dynamic-slice_bitcast_fusion.2), kind=kLoop, calls=%fused_computation.14.clone.1 | loop fusion | flops 31457280 | bytes 62939136 | tf_op jit(solution)/shard_map/while/body/eval_jaxpr/convert_element_type | solution.py:176
  462.6 16.1 %dynamic_update_slice.20 = f32[4,512,6,64]{1,0,3,2:T(4,128)} dynamic-update-slice(f32[4,512,6,64]{1,0,3,2:T(4,128)} %get-tuple-element.465, f32[1,512,6,64]{1,0,3,2:T(1,128)S(1)} %copy.134, s32[]{:T(128)} %get-tuple-element.462, s32[]{:T(128)} %constant.61.clone.1..sunk, s32[]{:T(128)} %constant.61.clone.1..sunk, s32[]{:T(128)} %constant.61.clone.1..sunk) | dynamic-update-slice | bytes 1572868 | tf_op jit(solution)/shard_map/while/body/jit(dynamic_update_index_in_dim)/dynamic_update_slice | solution.py:189
  515.1 17.3 %multiply_reduce_fusion.10 = (f32[6,512]{1,0:T(8,128)S(1)}, f32[6,512,2048]{2,1,0:T(8,128)}) fusion(f32[6,512,2048]{2,1,0:T(8,128)} %fusion.136, f32[6,512]{1,0:T(8,128)S(1)} %dynamic-slice_bitcast_fusion.2, bf16[2048,6,64]{0,2,1:T(8,128)(2,1)S(1)} %get-tuple-element.481, bf16[4,512,6,64]{1,3,2,0:T(8,128)(2,1)} %get-tuple-element.480, ...), kind=kOutput, calls=%fused_computation.15.clone.1 | convolution fusion | flops 830469120 | bytes 52322816 | tf_op jit(solution)/shard_map/while/body/eval_jaxpr/qhd,khd->hqk/dot_general | solution.py:172
  532.4 21.9 %multiply_convert_fusion.7 = bf16[6,512,2048]{2,1,0:T(8,128)(2,1)} fusion(f32[6,512,2048]{2,1,0:T(8,128)} %get-tuple-element.428, f32[6,512,2048]{2,1,0:T(8,128)} %fusion.136, f32[6,512]{1,0:T(8,128)S(1)} %get-tuple-element.429, f32[6,512]{1,0:T(8,128)S(1)} %dynamic-slice_bitcast_fusion.2), kind=kLoop, calls=%fused_computation.14.clone.1 | loop fusion | flops 31457280 | bytes 62939136 | tf_op jit(solution)/shard_map/while/body/eval_jaxpr/convert_element_type | solution.py:176
  563.7 16.1 %dynamic_update_slice.20 = f32[4,512,6,64]{1,0,3,2:T(4,128)} dynamic-update-slice(f32[4,512,6,64]{1,0,3,2:T(4,128)} %get-tuple-element.465, f32[1,512,6,64]{1,0,3,2:T(1,128)S(1)} %copy.134, s32[]{:T(128)} %get-tuple-element.462, s32[]{:T(128)} %constant.61.clone.1..sunk, s32[]{:T(128)} %constant.61.clone.1..sunk, s32[]{:T(128)} %constant.61.clone.1..sunk) | dynamic-update-slice | bytes 1572868 | tf_op jit(solution)/shard_map/while/body/jit(dynamic_update_index_in_dim)/dynamic_update_slice | solution.py:189
  589.4 15.6 %bitcast_add_fusion.5 = f32[2048,6,64]{0,2,1:T(8,128)} fusion(f32[2048,6,64]{0,2,1:T(8,128)} %get-tuple-element.464, f32[6,512,2048]{2,1,0:T(8,128)} %fusion.136, f32[6,512]{1,0:T(8,128)S(1)} %dynamic-slice_bitcast_fusion.2, pred[]{:T(512)S(6)} %compare.3, bf16[4,512,6,64]{1,3,2,0:T(8,128)(2,1)} %get-tuple-element.480, s32[]{:T(128)} %get-tuple-element.462), kind=kOutput, calls=%fused_computation.21.clone.1 | convolution fusion | flops 825753600 | bytes 31863296 | tf_op jit(solution)/shard_map/while/body/eval_jaxpr/hqk,qhd->khd/dot_general | solution.py:169
  616.8 16.3 %multiply_reduce_fusion.10 = (f32[6,512]{1,0:T(8,128)S(1)}, f32[6,512,2048]{2,1,0:T(8,128)}) fusion(f32[6,512,2048]{2,1,0:T(8,128)} %fusion.136, f32[6,512]{1,0:T(8,128)S(1)} %dynamic-slice_bitcast_fusion.2, bf16[2048,6,64]{0,2,1:T(8,128)(2,1)S(1)} %get-tuple-element.481, bf16[4,512,6,64]{1,3,2,0:T(8,128)(2,1)} %get-tuple-element.480, ...), kind=kOutput, calls=%fused_computation.15.clone.1 | convolution fusion | flops 830469120 | bytes 52322816 | tf_op jit(solution)/shard_map/while/body/eval_jaxpr/qhd,khd->hqk/dot_general | solution.py:172
  633.1 21.5 %multiply_convert_fusion.7 = bf16[6,512,2048]{2,1,0:T(8,128)(2,1)} fusion(f32[6,512,2048]{2,1,0:T(8,128)} %get-tuple-element.428, f32[6,512,2048]{2,1,0:T(8,128)} %fusion.136, f32[6,512]{1,0:T(8,128)S(1)} %get-tuple-element.429, f32[6,512]{1,0:T(8,128)S(1)} %dynamic-slice_bitcast_fusion.2), kind=kLoop, calls=%fused_computation.14.clone.1 | loop fusion | flops 31457280 | bytes 62939136 | tf_op jit(solution)/shard_map/while/body/eval_jaxpr/convert_element_type | solution.py:176
  664.0 16.1 %dynamic_update_slice.20 = f32[4,512,6,64]{1,0,3,2:T(4,128)} dynamic-update-slice(f32[4,512,6,64]{1,0,3,2:T(4,128)} %get-tuple-element.465, f32[1,512,6,64]{1,0,3,2:T(1,128)S(1)} %copy.134, s32[]{:T(128)} %get-tuple-element.462, s32[]{:T(128)} %constant.61.clone.1..sunk, s32[]{:T(128)} %constant.61.clone.1..sunk, s32[]{:T(128)} %constant.61.clone.1..sunk) | dynamic-update-slice | bytes 1572868 | tf_op jit(solution)/shard_map/while/body/jit(dynamic_update_index_in_dim)/dynamic_update_slice | solution.py:189
  689.6 15.6 %bitcast_add_fusion.5 = f32[2048,6,64]{0,2,1:T(8,128)} fusion(f32[2048,6,64]{0,2,1:T(8,128)} %get-tuple-element.464, f32[6,512,2048]{2,1,0:T(8,128)} %fusion.136, f32[6,512]{1,0:T(8,128)S(1)} %dynamic-slice_bitcast_fusion.2, pred[]{:T(512)S(6)} %compare.3, bf16[4,512,6,64]{1,3,2,0:T(8,128)(2,1)} %get-tuple-element.480, s32[]{:T(128)} %get-tuple-element.462), kind=kOutput, calls=%fused_computation.21.clone.1 | convolution fusion | flops 825753600 | bytes 31863296 | tf_op jit(solution)/shard_map/while/body/eval_jaxpr/hqk,qhd->khd/dot_general | solution.py:169
  717.1 16.3 %multiply_reduce_fusion.10 = (f32[6,512]{1,0:T(8,128)S(1)}, f32[6,512,2048]{2,1,0:T(8,128)}) fusion(f32[6,512,2048]{2,1,0:T(8,128)} %fusion.136, f32[6,512]{1,0:T(8,128)S(1)} %dynamic-slice_bitcast_fusion.2, bf16[2048,6,64]{0,2,1:T(8,128)(2,1)S(1)} %get-tuple-element.481, bf16[4,512,6,64]{1,3,2,0:T(8,128)(2,1)} %get-tuple-element.480, ...), kind=kOutput, calls=%fused_computation.15.clone.1 | convolution fusion | flops 830469120 | bytes 52322816 | tf_op jit(solution)/shard_map/while/body/eval_jaxpr/qhd,khd->hqk/dot_general | solution.py:172
  733.4 21.5 %multiply_convert_fusion.7 = bf16[6,512,2048]{2,1,0:T(8,128)(2,1)} fusion(f32[6,512,2048]{2,1,0:T(8,128)} %get-tuple-element.428, f32[6,512,2048]{2,1,0:T(8,128)} %fusion.136, f32[6,512]{1,0:T(8,128)S(1)} %get-tuple-element.429, f32[6,512]{1,0:T(8,128)S(1)} %dynamic-slice_bitcast_fusion.2), kind=kLoop, calls=%fused_computation.14.clone.1 | loop fusion | flops 31457280 | bytes 62939136 | tf_op jit(solution)/shard_map/while/body/eval_jaxpr/convert_element_type | solution.py:176
  764.2 16.1 %dynamic_update_slice.20 = f32[4,512,6,64]{1,0,3,2:T(4,128)} dynamic-update-slice(f32[4,512,6,64]{1,0,3,2:T(4,128)} %get-tuple-element.465, f32[1,512,6,64]{1,0,3,2:T(1,128)S(1)} %copy.134, s32[]{:T(128)} %get-tuple-element.462, s32[]{:T(128)} %constant.61.clone.1..sunk, s32[]{:T(128)} %constant.61.clone.1..sunk, s32[]{:T(128)} %constant.61.clone.1..sunk) | dynamic-update-slice | bytes 1572868 | tf_op jit(solution)/shard_map/while/body/jit(dynamic_update_index_in_dim)/dynamic_update_slice | solution.py:189
  789.9 15.6 %bitcast_add_fusion.5 = f32[2048,6,64]{0,2,1:T(8,128)} fusion(f32[2048,6,64]{0,2,1:T(8,128)} %get-tuple-element.464, f32[6,512,2048]{2,1,0:T(8,128)} %fusion.136, f32[6,512]{1,0:T(8,128)S(1)} %dynamic-slice_bitcast_fusion.2, pred[]{:T(512)S(6)} %compare.3, bf16[4,512,6,64]{1,3,2,0:T(8,128)(2,1)} %get-tuple-element.480, s32[]{:T(128)} %get-tuple-element.462), kind=kOutput, calls=%fused_computation.21.clone.1 | convolution fusion | flops 825753600 | bytes 31863296 | tf_op jit(solution)/shard_map/while/body/eval_jaxpr/hqk,qhd->khd/dot_general | solution.py:169
  836.8 73.2 %all_to_all.60 = bf16[2048,3,1,384]{3,1,2,0:T(4,128)(2,1)S(1)} all-to-all(bf16[2048,3,1,384]{3,1,2,0:T(4,128)(2,1)} %copy.112), channel_id=1, replica_groups=mesh['dp'=16,'seq'=2] {'seq'}, dimensions={0} | all-to-all | bytes 9437184 | tf_op jit(solution)/shard_map/all_to_all | solution.py:202
  946.2 30.9 %all-reduce.4 = (bf16[768]{0:T(1024)(128)(2,1)S(1)}, bf16[768]{0:T(1024)(128)(2,1)S(1)}) all-reduce(f32[768]{0:T(1024)S(1)} %get-tuple-element.250, f32[768]{0:T(1024)S(1)} %copy-done.26), channel_id=2, replica_groups=mesh['dp'=16,'seq'=2] {'dp'}, use_global_device_ids=true, to_apply=%region_16.17.clone | all-reduce | flops 1536 | bytes 9216
  988.2 28.6 %reduce-scatter.5.cloned.1.call-done = f32[48,2304]{1,0:T(8,128)} async-done(((f32[768,2304]{1,0:T(8,128)}), f32[48,2304]{1,0:T(8,128)}) %reduce-scatter.5.cloned.1.call-update) | async-done | bytes 442384 | tf_op jit(solution)/shard_map/reduce_scatter | solution.py:213
  1027.7 23.3 %all-reduce.10.cloned.1.call-done = (bf16[48,2304]{1,0:T(8,128)(2,1)}, bf16[48,768]{1,0:T(8,128)(2,1)}, bf16[48,2304]{1,0:T(8,128)(2,1)}, bf16[72,768]{1,0:T(8,128)(2,1)}) async-done(((bf16[48,2304]{1,0:T(8,128)(2,1)}, bf16[48,768]{1,0:T(8,128)(2,1)}, bf16[48,2304]{1,0:T(8,128)(2,1)}, bf16[72,768]{1,0:T(8,128)(2,1)}), (bf16[48,2304]{1,0:T(8,128)(2,1)}, bf16[48,768]{1,0:T(8,128)(2,1)}, ...) | async-done | bytes 626704 | tf_op jit(solution)/shard_map/psum | solution.py:221
  (245 shorter events, 521.3 us)
Async XLA Ops:
  7.2 53.0 %all-gather.5.cloned.1.call-start = ((), (), s32[]{:S(2)}) async-start(), calls=%async_computation.8 | async-start | bytes 3760128 | tf_op jit(solution)/shard_map/all_gather | solution.py:64
  7.9 295.2 %all-gather.7.cloned.1.call-start = ((), (), s32[]{:S(2)}) async-start(), calls=%async_computation.9 | async-start | bytes 1253376 | tf_op jit(solution)/shard_map/all_gather | solution.py:65
  8.7 299.8 %all-gather.9.cloned.1.call-start = ((), (), s32[]{:S(2)}) async-start(), calls=%async_computation.10 | async-start | bytes 3760128 | tf_op jit(solution)/shard_map/all_gather | solution.py:67
  11.2 55.3 %copy-start.5 = (bf16[1024,768]{0,1:T(8,128)(2,1)}, bf16[1024,768]{0,1:T(8,128)(2,1)S(1)}, u32[]{:S(2)}) copy-start(bf16[1024,768]{0,1:T(8,128)(2,1)S(1)} %copy.97) | copy-start | bytes 4718596
  49.0 17.5 %copy-start.22 = (f32[768]{0:T(1024)}, f32[768]{0:T(1024)S(1)}, u32[]{:S(2)}) copy-start(f32[768]{0:T(1024)S(1)} %convert_element_type.123) | copy-start | bytes 9220
  50.9 15.6 %copy-start.20 = (f32[1024]{0:T(1024)}, f32[1024]{0:T(1024)S(1)}, u32[]{:S(2)}) copy-start(f32[1024]{0:T(1024)S(1)} %broadcast_multiply_fusion.7) | copy-start | bytes 12292
  51.4 15.2 %copy-start.24 = (f32[1024]{0:T(1024)}, f32[1024]{0:T(1024)S(1)}, u32[]{:S(2)}) copy-start(f32[1024]{0:T(1024)S(1)} %add_rsqrt_fusion.1) | copy-start | bytes 12292
  74.4 59.5 %all-to-all-start = ((bf16[1024,3,2,384]{0,3,1,2:T(8,128)(2,1)}), bf16[1024,3,2,384]{0,3,1,2:T(8,128)(2,1)}, u32[]{:S(2)}, u32[]{:S(2)}) async-start(bf16[1024,3,2,384]{0,3,1,2:T(8,128)(2,1)} %copy.99), calls=%async_computation | async-start | bytes 9437184 | tf_op jit(solution)/shard_map/all_to_all | solution.py:86
  80.2 239.1 %all-gather.11.cloned.1.call-start = ((), (), s32[]{:S(2)}) async-start(), calls=%async_computation.11 | async-start | bytes 1880064 | tf_op jit(solution)/shard_map/all_gather | solution.py:68
  164.5 8.3 copy-start
  273.8 22.9 %all-to-all-start.1 = ((bf16[2,2,196608]{2,1,0:T(2,128)(2,1)}), bf16[2,2,196608]{2,1,0:T(2,128)(2,1)S(1)}, u32[]{:S(2)}, u32[]{:S(2)}) async-start(bf16[2,2,196608]{2,1,0:T(2,128)(2,1)} %reshape.424), calls=%async_computation.1 | async-start | bytes 3145728 | tf_op jit(solution)/shard_map/all_to_all | solution.py:114
  277.5 705.8 %reduce-scatter.7.cloned.1.call-start = ((), (), s32[]{:S(2)}) async-start(), calls=%async_computation.13 | async-start | bytes 2506752 | tf_op jit(solution)/shard_map/reduce_scatter | solution.py:214
  308.5 10.8 %copy-start.18 = (bf16[1024,768]{1,0:T(8,128)(2,1)S(1)}, bf16[1024,768]{1,0:T(8,128)(2,1)}, u32[]{:S(2)}) copy-start(bf16[1024,768]{1,0:T(8,128)(2,1)} %param.19) | copy-start | bytes 4718596
  319.3 16.1 %copy-start.12 = (f32[1024,2304]{1,0:T(8,128)S(1)}, f32[1024,2304]{1,0:T(8,128)}, u32[]{:S(2)}) copy-start(f32[1024,2304]{1,0:T(8,128)} %fusion.80) | copy-start | bytes 28311556
  351.7 633.2 %reduce-scatter.11.cloned.1.call-start = ((), (), s32[]{:S(2)}) async-start(), calls=%async_computation.15 | async-start | bytes 3760128 | tf_op jit(solution)/shard_map/reduce_scatter | solution.py:217
  366.1 23.1 %all-to-all-start.2 = ((bf16[1024,2,384]{0,2,1:T(8,128)(2,1)}), bf16[1024,2,384]{0,2,1:T(8,128)(2,1)}, u32[]{:S(2)}, u32[]{:S(2)}) async-start(bf16[1024,2,384]{0,2,1:T(8,128)(2,1)} %bitcast.183), calls=%async_computation.2 | async-start | bytes 3145728 | tf_op jit(solution)/shard_map/all_to_all | solution.py:155
  370.8 615.7 %reduce-scatter.9.cloned.1.call-start = ((), (), s32[]{:S(2)}) async-start(), calls=%async_computation.14 | async-start | bytes 7520256 | tf_op jit(solution)/shard_map/reduce_scatter | solution.py:216
  380.0 636.8 %reduce-scatter.5.cloned.1.call-start = ((), (), s32[]{:S(2)}) async-start(), calls=%async_computation.12 | async-start | bytes 7520256 | tf_op jit(solution)/shard_map/reduce_scatter | solution.py:213
  487.4 15.4 %copy-start.4 = (bf16[2048,6,64]{0,2,1:T(8,128)(2,1)S(1)}, bf16[2048,6,64]{0,2,1:T(8,128)(2,1)}, u32[]{:S(2)}) copy-start(bf16[2048,6,64]{0,2,1:T(8,128)(2,1)} %get-tuple-element.513) | copy-start | bytes 4718596 | tf_op jit(solution)/shard_map/while
  589.4 15.6 %copy-start.4 = (bf16[2048,6,64]{0,2,1:T(8,128)(2,1)S(1)}, bf16[2048,6,64]{0,2,1:T(8,128)(2,1)}, u32[]{:S(2)}) copy-start(bf16[2048,6,64]{0,2,1:T(8,128)(2,1)} %get-tuple-element.513) | copy-start | bytes 4718596 | tf_op jit(solution)/shard_map/while
  689.6 15.6 %copy-start.4 = (bf16[2048,6,64]{0,2,1:T(8,128)(2,1)S(1)}, bf16[2048,6,64]{0,2,1:T(8,128)(2,1)}, u32[]{:S(2)}) copy-start(bf16[2048,6,64]{0,2,1:T(8,128)(2,1)} %get-tuple-element.513) | copy-start | bytes 4718596 | tf_op jit(solution)/shard_map/while
  789.9 15.6 %copy-start.4 = (bf16[2048,6,64]{0,2,1:T(8,128)(2,1)S(1)}, bf16[2048,6,64]{0,2,1:T(8,128)(2,1)}, u32[]{:S(2)}) copy-start(bf16[2048,6,64]{0,2,1:T(8,128)(2,1)} %get-tuple-element.513) | copy-start | bytes 4718596 | tf_op jit(solution)/shard_map/while
  928.0 122.9 %all-reduce.10.cloned.1.call-start = ((), (), s32[]{:S(2)}) async-start(), calls=%async_computation.16 | async-start | bytes 1253376 | tf_op jit(solution)/shard_map/psum | solution.py:221
  936.2 10.0 copy-start.26
  (28 other events, 133.3 us)
Sparse Core Ops, SparseCore 0:
  10.3 49.8 all-gather.4
  62.5 37.4 all-gather.6
  102.3 46.0 all-gather.8
  150.4 39.3 all-gather.10
  351.8 61.1 reduce-scatter.6
  417.2 67.0 reduce-scatter.10
  488.9 88.9 reduce-scatter.8
  928.2 88.5 reduce-scatter.4
  1020.0 30.8 all-reduce.9
where the time goes:
time: 1080 us; the launch traced here: 1060 us
  matrix products  404 us (37%)
  local copies, waits for them, and re-layouts  197 us (18%)
  other arithmetic  152 us (14%)
  blocking collectives  145 us (13%)
  waiting for transfers between devices  134 us (12%)
  between operations  16.2 us (2%)
  starting transfers between devices  14.7 us (1%)
    convert_element_type x4, other arithmetic, backward_block(): grad_scores = (probs * (grad_probs - row_dot)).astype(jnp.bfloat16)  87.6 us
    all_to_all x1, blocking collectives, body(): lax.all_to_all(grad_heads.reshape(seq_len, 3, 1, head_cols), 'seq', split...  73.2 us
    dynamic_update_slice x8, local copies, waits for them, and re-layouts, body(): lax.scan(backward_block, (zero_heads, zero_heads), (q_blocks, grad_ctx_bl...  67.6 us
    unnamed x2, blocking collectives  66.9 us
    dot_general x4, matrix products, backward_block(): jnp.einsum('qhd,khd->hqk', g_block, value_rows, preferred_element_type=jn...  66.8 us
    dot_general x4, matrix products, backward_block(): jnp.einsum('hqk,qhd->khd', probs_low, g_block, preferred_element_type=jnp...  62 us
    all_to_all x1, waiting for transfers between devices, body(): lax.all_to_all(rotated.reshape(tok_rows, 3, ways, head_cols), 'seq', spli...  53.1 us
    dot_general x4, matrix products, forward_block(): jnp.einsum('hqk,khd->qhd', probs, value_rows, preferred_element_type=jnp....  48.2 us
  transfers between devices with their start and end apart: 12, of which 6 were waited for; matrix products, arithmetic and copies ran while one was open for 65% of the time, Pallas kernels for 0%

commit v1 on v0

v1 whole, which is shorter than its diff:
```python
import functools

import jax
import jax.numpy as jnp
from jax import lax
from jax.experimental import pallas as pl
from jax.experimental.pallas import tpu as pltpu
from jax.sharding import PartitionSpec as P

D = 768
HEADS = 12
HEAD_DIM = 64
FF = 1152
PAIR = 2 * HEAD_DIM
PAIRS = HEADS // 2

eps = 1e-05
rope_base = 160000.0
LIMIT = 56 * 1024 * 1024
BF = jnp.bfloat16
F32 = jnp.float32


def normalize_rows(values_in, gain_vec):
    centre = values_in - jnp.mean(values_in, axis=-1, keepdims=True)
    spread = jnp.mean(centre * centre, axis=-1, keepdims=True)
    inv_std = lax.rsqrt(spread + eps)
    unit_rows = centre * inv_std
    return (unit_rows * gain_vec, unit_rows, inv_std)


def normalize_back(grad_normed, gain_vec, unit_rows, inv_std):
    grad_unit = grad_normed * gain_vec
    return inv_std * (
        grad_unit
        - jnp.mean(grad_unit, axis=-1, keepdims=True)
        - unit_rows * jnp.mean(grad_unit * unit_rows, axis=-1, keepdims=True)
    )


def rotary_tables(positions):
    half_dim = HEAD_DIM // 2
    inverse = rope_base ** (-(jnp.arange(half_dim).astype(F32) * 2.0) / HEAD_DIM)
    phases = positions[:, None] * inverse[None, :]
    cos_half, sin_half = jnp.cos(phases), jnp.sin(phases)
    return (
        jnp.concatenate([cos_half] * 4, axis=-1),
        jnp.concatenate([-sin_half, sin_half] * 2, axis=-1),
    )


def turn(u, cos_table, sin_table):
    width = u.shape[-1]
    half = HEAD_DIM // 2
    lane = lax.broadcasted_iota(jnp.int32, u.shape, 1)
    from_right = pltpu.roll(u, width - half, 1)
    from_left = pltpu.roll(u, half, 1)
    other = jnp.where((lane & half) == 0, from_right, from_left)
    return u * cos_table + other * sin_table


def dot(a, b, a_dim, b_dim):
    return lax.dot_general(a, b, (((a_dim,), (b_dim,)), ((), ())), preferred_element_type=F32)


def project_kernel(turned_blocks, factor, act_ref, w_ref, cos_ref, sin_ref, out_ref):
    u = dot(act_ref[...], w_ref[...], 1, 0)
    wide = u.shape[-1] // PAIR

    @pl.when(pl.program_id(0) < turned_blocks)
    def _():
        cos_table = jnp.concatenate([cos_ref[...]] * wide, axis=-1)
        sin_table = jnp.concatenate([sin_ref[...]] * wide, axis=-1)
        out_ref[...] = turn(u, cos_table, sin_table).astype(BF) * jnp.array(factor, BF)

    @pl.when(pl.program_id(0) >= turned_blocks)
    def _():
        out_ref[...] = u.astype(BF)


def project(act, weight, cos_table, sin_table, first, columns, turned, factor):
    rows = act.shape[0]
    wide = 256
    return pl.pallas_call(
        functools.partial(project_kernel, turned // wide, factor),
        grid=(columns // wide,),
        in_specs=[
            pl.BlockSpec((rows, D), lambda c: (0, 0)),
            pl.BlockSpec((D, wide), lambda c: (0, first // wide + c)),
            pl.BlockSpec((rows, PAIR), lambda c: (0, 0)),
            pl.BlockSpec((rows, PAIR), lambda c: (0, 0)),
        ],
        out_specs=pl.BlockSpec((rows, wide), lambda c: (0, c)),
        out_shape=jax.ShapeDtypeStruct((rows, columns), BF),
        compiler_params=pltpu.CompilerParams(vmem_limit_bytes=LIMIT),
        cost_estimate=pl.CostEstimate(
            flops=2 * rows * D * columns, bytes_accessed=4 * rows * D, transcendentals=0
        ),
    )(act, weight, cos_table, sin_table)


def lanes_of(head, rows):
    lane = lax.broadcasted_iota(jnp.int32, (rows, PAIR), 1)
    return (lane < HEAD_DIM) if head == 0 else (lane >= HEAD_DIM)


def low_mask(head):
    return lanes_of(head, 1).astype(F32).astype(BF)


def forward_kernel(last, block, *refs):
    if last:
        q_ref, k_ref, v_ref, o_in, m_in, l_in, ctx_ref, lse_ref = refs
    else:
        q_ref, k_ref, v_ref, o_ref, m_ref, l_ref = refs
    keys = k_ref[...]
    masks = [low_mask(0), low_mask(1)]
    ones = jnp.ones((1, PAIR), BF)
    values = [v_ref[...] * mask + (ones - mask) for mask in masks]
    left = lanes_of(0, block)
    for start in range(0, q_ref.shape[0], block):
        rows = pl.ds(start, block)
        q_rows = q_ref[rows, :]
        tops, outs = [], []
        for head in range(2):
            scores = dot(q_rows * masks[head], keys, 1, 1)
            top = jnp.max(scores, axis=-1, keepdims=True)
            if last:
                top = jnp.maximum(top, m_in[rows, head * HEAD_DIM : head * HEAD_DIM + 1])
            tops.append(top)
            outs.append(dot(jnp.exp(scores - top).astype(BF), values[head], 1, 0))
        top = jnp.where(left, tops[0], tops[1])
        out = jnp.where(left, outs[0], outs[1])
        total = pltpu.roll(jnp.where(left, outs[1], outs[0]), HEAD_DIM, 1)
        if last:
            kept = jnp.exp(m_in[rows, :] - top)
            out = out + kept * o_in[rows, :]
            total = total + kept * l_in[rows, :]
            ctx_ref[rows, :] = (out / total).astype(BF)
            lse_ref[rows, :] = top + jnp.log(total)
        else:
            o_ref[rows, :] = out
            m_ref[rows, :] = top
            l_ref[rows, :] = total


def pair_spec(rows, shift=0):
    return pl.BlockSpec((rows, PAIR), lambda p: (0, p + shift))


def attend_cost(rows, products):
    return pl.CostEstimate(
        flops=2 * rows * rows * 2 * PAIR * HEADS * products,
        bytes_accessed=rows * D * 24,
        transcendentals=rows * rows * HEADS,
    )


def forward(queries, kv, carried):
    rows = queries.shape[0]
    last = carried is not None
    wide = jax.ShapeDtypeStruct((rows, D), F32)
    shapes = [jax.ShapeDtypeStruct((rows, D), BF), wide] if last else [wide, wide, wide]
    return pl.pallas_call(
        functools.partial(forward_kernel, last, 256),
        grid=(PAIRS,),
        in_specs=[pair_spec(rows), pair_spec(rows), pair_spec(rows, PAIRS)]
        + [pair_spec(rows)] * (3 if last else 0),
        out_specs=[pair_spec(rows)] * len(shapes),
        out_shape=shapes,
        compiler_params=pltpu.CompilerParams(vmem_limit_bytes=LIMIT),
        cost_estimate=attend_cost(rows, 2),
    )(queries, kv, kv, *(carried or ()))


def split_three(values_in):
    hi = values_in.astype(BF).astype(F32)
    rest = values_in - hi
    mid = rest.astype(BF).astype(F32)
    return hi, mid, rest - mid


def backward_kernel(last, block, *refs):
    if last:
        (q_ref, k_ref, v_ref, g_ref, ctx_ref, lse_ref, cos_ref, sin_ref, dq_in) = refs[:9]
        dq_ref, dk_ref, dv_ref, qa_ref, ga_ref, sum_ref = refs[9:]
    else:
        (q_ref, k_ref, v_ref, g_ref, ctx_ref, lse_ref, cos_ref, sin_ref) = refs[:8]
        dq_ref, dk_ref, dv_ref, qa_ref, ga_ref, sum_ref = refs[8:]
    count = q_ref.shape[0]
    queries = q_ref[...]
    grads = g_ref[...]
    product = grads.astype(F32) * ctx_ref[...].astype(F32)
    left = lanes_of(0, count)
    deltas = [
        jnp.sum(jnp.where(lanes_of(head, count), product, 0.0), axis=-1, keepdims=True)
        for head in range(2)
    ]
    log_parts = split_three(-pltpu.roll(lse_ref[...], HEAD_DIM, 1))
    delta_parts = split_three(-jnp.where(left, deltas[1], deltas[0]))
    lane = lax.broadcasted_iota(jnp.int32, (count, PAIR), 1)
    spot = lane & (HEAD_DIM - 1)

    def beside(own, base, parts):
        extra = jnp.where(spot == 0, parts[0], jnp.where(spot == 1, parts[1], parts[2]))
        extra = jnp.where(spot < 3, extra, 0.0)
        return jnp.where(own, base.astype(F32), extra).astype(BF)

    one_spot = ((lax.broadcasted_iota(jnp.int32, (1, PAIR), 1) & (HEAD_DIM - 1)) < 3).astype(F32)
    one_spot = one_spot.astype(BF)
    masks = [low_mask(0), low_mask(1)]
    ones = jnp.ones((1, PAIR), BF)
    for head in range(2):
        own = lanes_of(head, count)
        qa_ref[head] = beside(own, queries, log_parts)
        ga_ref[head] = beside(own, grads, delta_parts)
    left_block = lanes_of(0, block)
    for start in range(0, k_ref.shape[0], block):
        rows = pl.ds(start, block)
        k_rows, v_rows = k_ref[rows, :], v_ref[rows, :]
        dks, dvs = [], []
        for head in range(2):
            extra = (ones - masks[head]) * one_spot
            probs = jnp.exp(dot(k_rows * masks[head] + extra, qa_ref[head], 1, 1))
            centred = dot(v_rows * masks[head] + extra, ga_ref[head], 1, 1)
            dvs.append(dot(probs.astype(BF), grads, 1, 0))
            turned = (probs * centred).astype(BF)
            dks.append(dot(turned, queries, 1, 0))
            part = dot(turned, k_rows, 0, 0)
            if start == 0:
                sum_ref[head] = part
            else:
                sum_ref[head] += part
        dk = jnp.where(left_block, dks[0], dks[1])
        dk_ref[rows, :] = turn(dk, cos_ref[rows, :], -sin_ref[rows, :]).astype(BF)
        dv_ref[rows, :] = jnp.where(left_block, dvs[0], dvs[1]).astype(BF)
    dq = jnp.where(left, sum_ref[0], sum_ref[1]) * (HEAD_DIM**-0.5)
    if last:
        dq = dq + dq_in[...]
        dq_ref[...] = turn(dq, cos_ref[...], -sin_ref[...]).astype(BF)
    else:
        dq_ref[...] = dq


def backward(queries, kv, grads, ctx, lse, cos_table, sin_table, carried):
    rows = queries.shape[0]
    last = carried is not None
    low = jax.ShapeDtypeStruct((rows, D), BF)
    table = pl.BlockSpec((rows, PAIR), lambda p: (0, 0))
    args = [queries, kv, kv, grads, ctx, lse, cos_table, sin_table]
    specs = [pair_spec(rows), pair_spec(rows), pair_spec(rows, PAIRS)]
    specs += [pair_spec(rows)] * 3 + [table, table]
    if last:
        args.append(carried)
        specs.append(pair_spec(rows))
    return pl.pallas_call(
        functools.partial(backward_kernel, last, 256),
        grid=(PAIRS,),
        in_specs=specs,
        out_specs=[pair_spec(rows)] * 3,
        out_shape=[low if last else jax.ShapeDtypeStruct((rows, D), F32), low, low],
        scratch_shapes=[
            pltpu.VMEM((2, rows, PAIR), BF),
            pltpu.VMEM((2, rows, PAIR), BF),
            pltpu.VMEM((2, rows, PAIR), F32),
        ],
        compiler_params=pltpu.CompilerParams(vmem_limit_bytes=LIMIT),
        cost_estimate=attend_cost(rows, 5),
    )(*args)


def gated(gate_part, up_part):
    return jax.nn.gelu(gate_part, approximate=False) * up_part


def body(tokens, gain_attn, w_qkv, w_out, gain_mlp, w_in, w_down, d_out):
    ways = lax.axis_size("seq")
    tok_rows = tokens.shape[0]
    swap = [(i, (i + 1) % ways) for i in range(ways)]
    shard = gain_attn.shape[0]

    packed = jnp.concatenate(
        [w_qkv, gain_attn[:, None], gain_mlp[:, None], jnp.zeros((shard, PAIR - 2), BF)], axis=1
    )
    packed = lax.all_gather(packed, "dp", axis=0, tiled=True)
    full_out = lax.all_gather(w_out, "dp", axis=0, tiled=True)
    full_in = lax.all_gather(w_in, "dp", axis=0, tiled=True)
    full_down = lax.all_gather(w_down, "dp", axis=0, tiled=True)
    gain_one = packed[:, 3 * D].astype(F32)
    gain_two = packed[:, 3 * D + 1].astype(F32)

    here = lax.axis_index("seq")
    there = lax.rem(here + 1, ways)
    steps = jnp.arange(tok_rows)
    cos_here, sin_here = rotary_tables((here * tok_rows + steps).astype(F32))
    cos_there, sin_there = rotary_tables((there * tok_rows + steps).astype(F32))

    inputs = tokens.astype(F32)
    normed_one, unit_one, inv_one = normalize_rows(inputs, gain_one)
    act_one = normed_one.astype(BF)
    kv_here = project(act_one, packed, cos_here, sin_here, D, 2 * D, D, 1.0)
    kv_there = lax.ppermute(kv_here, "seq", swap)
    queries = project(act_one, packed, cos_here, sin_here, 0, D, D, HEAD_DIM**-0.5)
    partial = forward(queries, kv_here, None)
    ctx, lse = forward(queries, kv_there, partial)

    attended = jnp.dot(ctx, full_out, preferred_element_type=F32)
    hidden = inputs + attended
    normed_two, unit_two, inv_two = normalize_rows(hidden, gain_two)
    act_two = normed_two.astype(BF)
    gate_up = jnp.dot(act_two, full_in, preferred_element_type=F32)
    gated_value, gated_pull = jax.vjp(gated, gate_up[:, :FF], gate_up[:, FF:])
    activated = gated_value.astype(BF)
    mixed = (hidden + jnp.dot(activated, full_down, preferred_element_type=F32)).astype(BF)

    grad_out = d_out.astype(F32)
    grad_w_down = dot(activated, d_out, 0, 0)
    grad_act = dot(d_out, full_down, 1, 1)
    grad_gate, grad_up = gated_pull(grad_act)
    grad_gate_up = jnp.concatenate([grad_gate, grad_up], axis=1).astype(BF)
    grad_w_in = dot(act_two, grad_gate_up, 0, 0)
    grad_norm_two = dot(grad_gate_up, full_in, 1, 1)
    grad_hidden = grad_out + normalize_back(grad_norm_two, gain_two, unit_two, inv_two)
    grad_hidden_low = grad_hidden.astype(BF)
    grad_w_out = dot(ctx, grad_hidden_low, 0, 0)
    grad_ctx = dot(grad_hidden_low, full_out, 1, 1).astype(BF)

    dq_part, dk_far, dv_far = backward(
        queries, kv_there, grad_ctx, ctx, lse, cos_there, sin_there, None
    )
    dk_got = lax.ppermute(dk_far, "seq", swap)
    dv_got = lax.ppermute(dv_far, "seq", swap)
    dq, dk, dv = backward(queries, kv_here, grad_ctx, ctx, lse, cos_here, sin_here, dq_part)
    dk = (dk.astype(F32) + dk_got.astype(F32)).astype(BF)
    dv = (dv.astype(F32) + dv_got.astype(F32)).astype(BF)
    grad_proj = jnp.concatenate([dq, dk, dv], axis=1)

    grad_w_qkv = dot(act_one, grad_proj, 0, 0)
    full_qkv = packed[:, : 3 * D]
    grad_norm_one = dot(grad_proj, full_qkv, 1, 1)
    grad_tokens = grad_hidden + normalize_back(grad_norm_one, gain_one, unit_one, inv_one)

    def owned(grad):
        part = lax.psum_scatter(grad.astype(BF), "dp", scatter_dimension=0, tiled=True)
        other = lax.ppermute(part, "seq", swap)
        return part.astype(F32) + other.astype(F32)

    own_down, own_in, own_out, own_qkv = (
        owned(grad_w_down), owned(grad_w_in), owned(grad_w_out), owned(grad_w_qkv)
    )
    own_gain_one = jnp.sum(own_qkv * w_qkv.astype(F32), axis=1) / gain_attn.astype(F32)
    own_gain_two = jnp.sum(own_in * w_in.astype(F32), axis=1) / gain_mlp.astype(F32)
    return (
        mixed, grad_tokens, own_gain_one, own_qkv, own_out, own_gain_two, own_in, own_down
    )


def solution(mesh):
    in_specs = (
        P(("dp", "seq"), None),
        P("dp"),
        P("dp", None),
        P("dp", None),
        P("dp"),
        P("dp", None),
        P("dp", None),
        P(("dp", "seq"), None),
    )
    out_specs = (
        P(("dp", "seq"), None),
        P(("dp", "seq"), None),
        P("dp"),
        P("dp", None),
        P("dp", None),
        P("dp"),
        P("dp", None),
        P("dp", None),
    )
    return jax.shard_map(body, mesh=mesh, in_specs=in_specs, out_specs=out_specs, check_vma=False)
```

time: 1080 us -> 508 us (0.47); the launches traced: 1060 us -> 504 us
  matrix products: 404 us -> 74.7 us
  local copies, waits for them, and re-layouts: 197 us -> 12.2 us
  Pallas kernels: 0 us -> 161 us
  blocking collectives: 145 us -> 0 us
  other arithmetic: 152 us -> 33.7 us
  waiting for transfers between devices: 134 us -> 198 us
    dot_general x40 -> x11, matrix products: 404 us -> 74.7 us  [the longest x8 54 us: dot(): lax.dot_general(a, b, (((a_dim,), (b_dim,)), ((), ())), preferred_element...]
    pallas_call x0 -> x6, Pallas kernels: none -> 161 us  [the longest x2 86.7 us: backward(): pl.pallas_call(functools.partial(backward_kernel, last, 256), grid=(PAIRS...]
    convert_element_type x18 -> x6, other arithmetic: 102 us -> 5.34 us  [the longest x1 1.92 us: body(): dk = (dk.astype(F32) + dk_got.astype(F32)).astype(BF)]
    all_to_all x1 -> x0, blocking collectives: 73.2 us -> none  [body(): lax.all_to_all(grad_heads.reshape(seq_len, 3, 1, head_cols), 'seq', split...]
    all_to_all x3 -> x0, waiting for transfers between devices: 71.3 us -> none  [the longest x1 53.1 us: body(): lax.all_to_all(rotated.reshape(tok_rows, 3, ways, head_cols), 'seq', spli...]
    dynamic_update_slice x8 -> x0, local copies, waits for them, and re-layouts: 67.6 us -> none  [body(): lax.scan(backward_block, (zero_heads, zero_heads), (q_blocks, grad_ctx_bl...]
    unnamed x2 -> x0, blocking collectives: 66.9 us -> none
    ppermute x0 -> x7, waiting for transfers between devices: none -> 65.2 us  [the longest x1 36.2 us: body(): kv_there = lax.ppermute(kv_here, 'seq', swap)]
  transfers between devices with their start and end apart: 12 -> 15, of which waited for: 6 -> 7; matrix products, arithmetic and copies ran while one was open for 65% -> 15% of each run, Pallas kernels for 0% -> 32%
where the time goes in v1:
time: 508 us; the launch traced here: 504 us
  waiting for transfers between devices  198 us (39%)
  Pallas kernels  161 us (32%)
  matrix products  74.7 us (15%)
  other arithmetic  33.7 us (7%)
  between operations  15 us (3%)
  local copies, waits for them, and re-layouts  12.2 us (2%)
  starting transfers between devices  9.17 us (2%)
    reduce_scatter x4, waiting for transfers between devices, owned(): lax.psum_scatter(grad.astype(BF), 'dp', scatter_dimension=0, tiled=True)  89.9 us
    pallas_call x2, Pallas kernels, backward(): pl.pallas_call(functools.partial(backward_kernel, last, 256), grid=(PAIRS...  86.7 us
    pallas_call x2, Pallas kernels, forward(): pl.pallas_call(functools.partial(forward_kernel, last, 256), grid=(PAIRS,...  58.8 us
    dot_general x8, matrix products, dot(): lax.dot_general(a, b, (((a_dim,), (b_dim,)), ((), ())), preferred_element...  54 us
    all_gather x1, waiting for transfers between devices, body(): packed = lax.all_gather(packed, 'dp', axis=0, tiled=True)  41.4 us
    ppermute x1, waiting for transfers between devices, body(): kv_there = lax.ppermute(kv_here, 'seq', swap)  36.2 us
    ppermute x1, waiting for transfers between devices, body(): dv_got = lax.ppermute(dv_far, 'seq', swap)  21.8 us
    pallas_call x2, Pallas kernels, project(): pl.pallas_call(functools.partial(project_kernel, turned // wide, factor),...  15.8 us
  transfers between devices with their start and end apart: 15, of which 7 were waited for; matrix products, arithmetic and copies ran while one was open for 15% of the time, Pallas kernels for 32%

profile of v1, /device:TPU:0, one launch (start us, length us, event | category | flops | bytes accessed | tf_op | source)
XLA Modules:
  0.0 503.9 jit_solution(2587284209561378599)
XLA Ops:
  12.1 5.1 %fusion.24 = (f32[1024,32]{1,0:T(8,128)}, f32[1024,32]{1,0:T(8,128)}, f32[1024,32]{1,0:T(8,128)}, f32[1024,32]{1,0:T(8,128)S(1)}, f32[1024,32]{1,0:T(8,128)S(1)}, /*index=5*/f32[1024,32]{1,0:T(8,128)S(1)}) fusion(f32[32]{0:T(128)S(1)} %multiply_power_fusion, f32[1024]{0:T(1024)S(1)} %add_convert_fusion.4, f32[1024]{0:T(1024)S(1)} %add_convert_fusion.5), kind=kLoop, calls=%fused_computation.72 | loop fusion | flops 131072 | bytes 794752 | tf_op jit(solution)/shard_map/neg | solution.py:48
  20.0 41.4 %all-gather.5.cloned.1.call-done.w_ref = bf16[768,2432]{1,0:T(8,128)(2,1)} async-done(((bf16[48,2432]{1,0:T(8,128)(2,1)}), bf16[768,2432]{1,0:T(8,128)(2,1)}) %all-gather.5.cloned.1.call-update) | async-done | bytes 3735568 | tf_op jit(solution)/shard_map/all_gather | solution.py:285
  64.9 9.1 %shard_map.144.refs_1_.refs_2_ = bf16[1024,1536]{1,0:T(8,128)(2,1)} custom-call(bf16[1024,768]{1,0:T(8,128)(2,1)} %fusion.14.act_ref, bf16[768,2432]{1,0:T(8,128)(2,1)} %all-gather.5.cloned.1.call-done.w_ref, f32[1024,128]{1,0:T(8,128)} %get-tuple-element.58.cos_ref.refs_6_, f32[1024,128]{1,0:T(8,128)} %get-tuple-element.59.sin_ref.refs_7_), custom_call_target="tpu_custom_call" | custom-call | flops 2415919104 | bytes 3145728 | tf_op jit(solution)/shard_map/pallas_call | solution.py:84
  75.8 6.7 %shard_map.143.refs_0_ = bf16[1024,768]{1,0:T(8,128)(2,1)} custom-call(bf16[1024,768]{1,0:T(8,128)(2,1)} %fusion.14.act_ref, bf16[768,2432]{1,0:T(8,128)(2,1)} %all-gather.5.cloned.1.call-done.w_ref, f32[1024,128]{1,0:T(8,128)} %get-tuple-element.58.cos_ref.refs_6_, f32[1024,128]{1,0:T(8,128)} %get-tuple-element.59.sin_ref.refs_7_), custom_call_target="tpu_custom_call" | custom-call | flops 1207959552 | bytes 3145728 | tf_op jit(solution)/shard_map/pallas_call | solution.py:84
  82.6 25.9 %shard_map.145 = (f32[1024,768]{1,0:T(8,128)}, f32[1024,768]{1,0:T(8,128)}, f32[1024,768]{1,0:T(8,128)}) custom-call(bf16[1024,768]{1,0:T(8,128)(2,1)} %shard_map.143.refs_0_, bf16[1024,1536]{1,0:T(8,128)(2,1)} %shard_map.144.refs_1_.refs_2_, bf16[1024,1536]{1,0:T(8,128)(2,1)} %shard_map.144.refs_1_.refs_2_), custom_call_target="tpu_custom_call" | custom-call | flops 12884901888 | bytes 18874368 | tf_op jit(solution)/shard_map/pallas_call | solution.py:164
  108.4 36.2 %collective-permute-done.refs_1_.refs_2_ = bf16[1024,1536]{1,0:T(8,128)(2,1)} collective-permute-done((bf16[1024,1536]{1,0:T(8,128)(2,1)}, bf16[1024,1536]{1,0:T(8,128)(2,1)}, u32[]{:S(2)}, u32[]{:S(2)}) %collective-permute-start) | collective-permute-done | bytes 3145760 | tf_op jit(solution)/shard_map/ppermute | solution.py:302
  144.6 32.9 %shard_map.146 = (bf16[1024,768]{1,0:T(8,128)(2,1)}, f32[1024,768]{1,0:T(8,128)}) custom-call(bf16[1024,768]{1,0:T(8,128)(2,1)} %shard_map.143.refs_0_, bf16[1024,1536]{1,0:T(8,128)(2,1)} %collective-permute-done.refs_1_.refs_2_, bf16[1024,1536]{1,0:T(8,128)(2,1)} %collective-permute-done.refs_1_.refs_2_, f32[1024,768]{1,0:T(8,128)} %get-tuple-element.19.refs_3_, ...), custom_call_target="tpu_custom_call" | custom-call | flops 12884901888 | bytes 18874368 | tf_op jit(solution)/shard_map/pallas_call | solution.py:164
  183.1 10.7 %fusion.29 = f32[1024,2304]{1,0:T(8,128)} fusion(bf16[768,2304]{1,0:T(8,128)(2,1)} %all-gather.9.cloned.1.call-done, f32[1024,768]{1,0:T(8,128)} %copy-done.4, f32[768]{0:T(1024)S(1)} %get-tuple-element.30, f32[1024]{0:T(1024)S(1)} %add_rsqrt_fusion, f32[1024]{0:T(1024)S(1)} %broadcast_multiply_fusion.4), kind=kOutput, calls=%fused_computation.91 | convolution fusion | flops 3627024384 | bytes 16133120 | tf_op jit(solution)/shard_map/dot_general | solution.py:311
  193.8 16.1 %add_convert_fusion = (bf16[1024,1152]{1,0:T(8,128)(2,1)}, f32[1024,1152]{1,0:T(8,128)S(1)}, f32[1024,1152]{1,0:T(8,128)S(1)}) fusion(f32[1024,2304]{1,0:T(8,128)} %fusion.29, bf16[1024,768]{1,0:T(8,128)(2,1)S(1)} %copy-done.10, bf16[1152,768]{1,0:T(8,128)(2,1)} %all-gather.11.cloned.1.call-done), kind=kOutput, calls=%fused_computation.10 | convolution fusion | flops 1898053632 | bytes 24576000 | tf_op jit(solution)/shard_map/dot_general | solution.py:63
  214.5 6.0 %multiply_reduce_fusion.3 = (f32[1024]{0:T(1024)S(1)}, f32[1024]{0:T(1024)S(1)}, f32[1024,768]{1,0:T(8,128)S(1)}) fusion(f32[768]{0:T(1024)S(1)} %get-tuple-element.30, f32[1024]{0:T(1024)S(1)} %add_rsqrt_fusion, f32[1024,768]{1,0:T(8,128)S(1)} %copy-done.5, f32[1024]{0:T(1024)S(1)} %broadcast_multiply_fusion.4, bf16[768,2304]{1,0:T(8,128)(2,1)S(1)} %copy-done.26, ...), kind=kOutput, calls=%fused_computation.51 | convolution fusion | flops 3638032384 | bytes 14568448 | tf_op jit(solution)/shard_map/dot_general | solution.py:63
  226.2 5.4 %convolution_convert_fusion.2 = bf16[1152,768]{1,0:T(8,128)(2,1)} fusion(bf16[1024,1152]{1,0:T(8,128)(2,1)} %get-tuple-element.43, bf16[1024,768]{1,0:T(8,128)(2,1)} %param.15), kind=kOutput, calls=%fused_computation.34 | convolution fusion | flops 1812824064 | bytes 5701632 | tf_op jit(solution)/shard_map/dot_general | solution.py:63
  231.6 4.2 pad_maximum_fusion.8
  235.8 8.3 %convolution_convert_fusion = bf16[768,2304]{1,0:T(8,128)(2,1)} fusion(bf16[1024,1152]{1,0:T(8,128)(2,1)} %copy-done.9, bf16[1024,1152]{1,0:T(8,128)(2,1)} %get-tuple-element.40, f32[1024,768]{1,0:T(8,128)S(1)} %copy-done.5, f32[768]{0:T(1024)S(1)} %get-tuple-element.30, f32[1024]{0:T(1024)S(1)} %add_rsqrt_fusion, f32[1024]{0:T(1024)S(1)} %broadcast_multiply_fusion.4), kind=kOutput, calls=%fused_computation.1 | convolution fusion | flops 3638231040 | bytes 11414528 | tf_op jit(solution)/shard_map/dot_general | solution.py:63
  246.0 3.8 convolution_convert_fusion.3.refs_3_
  249.9 42.8 %shard_map.147 = (f32[1024,768]{1,0:T(8,128)}, bf16[1024,768]{1,0:T(8,128)(2,1)}, bf16[1024,768]{1,0:T(8,128)(2,1)}) custom-call(bf16[1024,768]{1,0:T(8,128)(2,1)} %shard_map.143.refs_0_, bf16[1024,1536]{1,0:T(8,128)(2,1)} %collective-permute-done.refs_1_.refs_2_, bf16[1024,1536]{1,0:T(8,128)(2,1)} %collective-permute-done.refs_1_.refs_2_, ...), custom_call_target="tpu_custom_call" | custom-call | flops 32212254720 | bytes 18874368 | tf_op jit(solution)/shard_map/pallas_call | solution.py:256
  294.7 43.9 %shard_map.148 = (bf16[1024,768]{1,0:T(8,128)(2,1)}, bf16[1024,768]{1,0:T(8,128)(2,1)}, bf16[1024,768]{1,0:T(8,128)(2,1)}) custom-call(bf16[1024,768]{1,0:T(8,128)(2,1)} %shard_map.143.refs_0_, bf16[1024,1536]{1,0:T(8,128)(2,1)} %shard_map.144.refs_1_.refs_2_, bf16[1024,1536]{1,0:T(8,128)(2,1)} %shard_map.144.refs_1_.refs_2_, ...), custom_call_target="tpu_custom_call" | custom-call | flops 32212254720 | bytes 18874368 | tf_op jit(solution)/shard_map/pallas_call | solution.py:256
  340.5 21.8 %collective-permute-done.2 = bf16[1024,768]{1,0:T(8,128)(2,1)S(1)} collective-permute-done((bf16[1024,768]{1,0:T(8,128)(2,1)}, bf16[1024,768]{1,0:T(8,128)(2,1)S(1)}, u32[]{:S(2)}, u32[]{:S(2)}) %collective-permute-start.2) | collective-permute-done | bytes 1572896 | tf_op jit(solution)/shard_map/ppermute | solution.py:332
  363.9 6.3 %convolution_convert_fusion.1 = bf16[768,2304]{1,0:T(8,128)(2,1)} fusion(bf16[1024,768]{1,0:T(8,128)(2,1)S(1)} %copy-done.3, bf16[1024,768]{1,0:T(8,128)(2,1)S(1)} %add_convert_fusion.1, bf16[1024,768]{1,0:T(8,128)(2,1)S(1)} %add_convert_fusion.2, bf16[1024,768]{1,0:T(8,128)(2,1)S(1)} %copy-done.28), kind=kOutput, calls=%fused_computation.2 | convolution fusion | flops 3639803904 | bytes 9830400 | tf_op jit(solution)/shard_map/dot_general | solution.py:63
  370.3 6.6 %add_convert_fusion.3 = bf16[1024,768]{1,0:T(8,128)(2,1)} fusion(f32[1024,768]{1,0:T(8,128)} %copy-done.4, bf16[1024,1152]{1,0:T(8,128)(2,1)} %get-tuple-element.43, bf16[1152,768]{1,0:T(8,128)(2,1)} %all-gather.11.cloned.1.call-done), kind=kOutput, calls=%fused_computation.45 | convolution fusion | flops 1813512192 | bytes 8847360 | tf_op jit(solution)/shard_map/dot_general | solution.py:314
  377.0 5.7 %multiply_reduce_fusion.2 = (f32[1024]{0:T(1024)S(1)}, f32[1024]{0:T(1024)S(1)}, f32[1024,768]{1,0:T(8,128)}) fusion(f32[768]{0:T(1024)S(1)} %copy-done.21, f32[1024]{0:T(1024)S(1)} %copy-done.23, f32[1024]{0:T(1024)S(1)} %copy-done.19, bf16[1024,768]{1,0:T(8,128)(2,1)S(1)} %copy-done.1, bf16[768,2432]{1,0:T(8,128)(2,1)S(1)} %copy-done.2, ...), kind=kOutput, calls=%fused_computation.50 | convolution fusion | flops 3643537408 | bytes 12996608 | tf_op jit(solution)/shard_map/dot_general | solution.py:63
  384.1 4.6 fusion.18
  390.0 27.2 %reduce-scatter.9.cloned.1.call-done = bf16[48,2304]{1,0:T(8,128)(2,1)} async-done(((bf16[768,2304]{1,0:T(8,128)(2,1)}), bf16[48,2304]{1,0:T(8,128)(2,1)}) %reduce-scatter.9.cloned.1.call-update) | async-done | bytes 221200 | tf_op jit(solution)/shard_map/reduce_scatter | solution.py:344
  425.3 62.7 %reduce-scatter.5.cloned.1.call-done = bf16[48,2304]{1,0:T(8,128)(2,1)} async-done(((bf16[768,2304]{1,0:T(8,128)(2,1)}), bf16[48,2304]{1,0:T(8,128)(2,1)}) %reduce-scatter.5.cloned.1.call-update) | async-done | bytes 221200 | tf_op jit(solution)/shard_map/reduce_scatter | solution.py:344
  490.1 4.1 collective-permute-done.3
  (125 shorter events, 51.4 us)
Async XLA Ops:
  7.2 54.2 %all-gather.5.cloned.1.call-start = ((), (), s32[]{:S(2)}) async-start(), calls=%async_computation.4 | async-start | bytes 3969024 | tf_op jit(solution)/shard_map/all_gather | solution.py:285
  10.5 167.1 %all-gather.7.cloned.1.call-start = ((), (), s32[]{:S(2)}) async-start(), calls=%async_computation.5 | async-start | bytes 1253376 | tf_op jit(solution)/shard_map/all_gather | solution.py:286
  11.2 171.8 %all-gather.9.cloned.1.call-start = ((), (), s32[]{:S(2)}) async-start(), calls=%async_computation.6 | async-start | bytes 3760128 | tf_op jit(solution)/shard_map/all_gather | solution.py:287
  12.0 181.9 %all-gather.11.cloned.1.call-start = ((), (), s32[]{:S(2)}) async-start(), calls=%async_computation.7 | async-start | bytes 1880064 | tf_op jit(solution)/shard_map/all_gather | solution.py:288
  19.3 54.7 %copy-start.18 = (f32[1024]{0:T(1024)}, f32[1024]{0:T(1024)S(1)}, u32[]{:S(2)}) copy-start(f32[1024]{0:T(1024)S(1)} %broadcast_multiply_fusion.5) | copy-start | bytes 12292
  19.9 54.1 %copy-start.22 = (f32[1024]{0:T(1024)}, f32[1024]{0:T(1024)S(1)}, u32[]{:S(2)}) copy-start(f32[1024]{0:T(1024)S(1)} %add_rsqrt_fusion.1) | copy-start | bytes 12292
  74.0 70.6 %collective-permute-start = (bf16[1024,1536]{1,0:T(8,128)(2,1)}, bf16[1024,1536]{1,0:T(8,128)(2,1)}, u32[]{:S(2)}, u32[]{:S(2)}) collective-permute-start(bf16[1024,1536]{1,0:T(8,128)(2,1)} %shard_map.144.refs_1_.refs_2_), channel_id=1, source_target_pairs={{0,1},{1,0},{2,3},{3,2},{4,5},{5,4},{6,7},{7,6},{8,9},{9,8},{10,11... | collective-permute-start | bytes 9437192 | tf_op jit(solution)/shard_map/ppermute | solution.py:302
  75.6 307.1 %reduce-scatter.7.cloned.1.call-start = ((), (), s32[]{:S(2)}) async-start(), calls=%async_computation.9 | async-start | bytes 1253376 | tf_op jit(solution)/shard_map/reduce_scatter | solution.py:344
  226.1 162.6 %reduce-scatter.11.cloned.1.call-start = ((), (), s32[]{:S(2)}) async-start(), calls=%async_computation.11 | async-start | bytes 1880064 | tf_op jit(solution)/shard_map/reduce_scatter | solution.py:344
  231.6 185.6 %reduce-scatter.9.cloned.1.call-start = ((), (), s32[]{:S(2)}) async-start(), calls=%async_computation.10 | async-start | bytes 3760128 | tf_op jit(solution)/shard_map/reduce_scatter | solution.py:344
  244.2 243.8 %reduce-scatter.5.cloned.1.call-start = ((), (), s32[]{:S(2)}) async-start(), calls=%async_computation.8 | async-start | bytes 3760128 | tf_op jit(solution)/shard_map/reduce_scatter | solution.py:344
  292.6 45.9 %collective-permute-start.1 = (bf16[1024,768]{1,0:T(8,128)(2,1)}, bf16[1024,768]{1,0:T(8,128)(2,1)S(1)}, u32[]{:S(2)}, u32[]{:S(2)}) collective-permute-start(bf16[1024,768]{1,0:T(8,128)(2,1)} %get-tuple-element.27), channel_id=1, source_target_pairs={{0,1},{1,0},{2,3},{3,2},{4,5},{5,4},{6,7},{7,6},{8,9},{9,8},{10,11... | collective-permute-start | bytes 4718600 | tf_op jit(solution)/shard_map/ppermute | solution.py:331
  294.1 68.3 %collective-permute-start.2 = (bf16[1024,768]{1,0:T(8,128)(2,1)}, bf16[1024,768]{1,0:T(8,128)(2,1)S(1)}, u32[]{:S(2)}, u32[]{:S(2)}) collective-permute-start(bf16[1024,768]{1,0:T(8,128)(2,1)} %get-tuple-element.29), channel_id=1, source_target_pairs={{0,1},{1,0},{2,3},{3,2},{4,5},{5,4},{6,7},{7,6},{8,9},{9,8},{10,11... | collective-permute-start | bytes 4718600 | tf_op jit(solution)/shard_map/ppermute | solution.py:332
  338.6 23.8 %copy-start.14 = (bf16[1024,768]{1,0:T(8,128)(2,1)S(1)}, bf16[1024,768]{1,0:T(8,128)(2,1)}, u32[]{:S(2)}) copy-start(bf16[1024,768]{1,0:T(8,128)(2,1)} %get-tuple-element.28) | copy-start | bytes 4718596
  340.5 23.4 %copy-start.3 = (bf16[1024,768]{1,0:T(8,128)(2,1)S(1)}, bf16[1024,768]{1,0:T(8,128)(2,1)}, u32[]{:S(2)}) copy-start(bf16[1024,768]{1,0:T(8,128)(2,1)} %fusion.14.act_ref) | copy-start | bytes 4718596
  340.5 23.4 %copy-start.28 = (bf16[1024,768]{1,0:T(8,128)(2,1)S(1)}, bf16[1024,768]{1,0:T(8,128)(2,1)}, u32[]{:S(2)}) copy-start(bf16[1024,768]{1,0:T(8,128)(2,1)} %get-tuple-element.25) | copy-start | bytes 4718596
  382.7 6.7 %collective-permute-start.4 = (bf16[48,768]{1,0:T(8,128)(2,1)}, bf16[48,768]{1,0:T(8,128)(2,1)S(1)}, u32[]{:S(2)}, u32[]{:S(2)}) collective-permute-start(bf16[48,768]{1,0:T(8,128)(2,1)} %reduce-scatter.7.cloned.1.call-done), channel_id=1, source_target_pairs={{0,1},{1,0},{2,3},{3,2},{4,5},{5,4},{6,7},{7,6},{8,9},{9,8},{10,11... | collective-permute-start | bytes 221192 | tf_op jit(solution)/shard_map/ppermute | solution.py:345
  384.1 39.2 %copy-start.15 = (bf16[48,2304]{1,0:T(8,128)(2,1)S(1)}, bf16[48,2304]{1,0:T(8,128)(2,1)}, u32[]{:S(2)}) copy-start(bf16[48,2304]{1,0:T(8,128)(2,1)} %param.13) | copy-start | bytes 663556
  384.1 105.4 %copy-start.24 = (bf16[48]{0:T(256)(128)(2,1)S(1)}, bf16[48]{0:T(256)(128)(2,1)}, u32[]{:S(2)}) copy-start(bf16[48]{0:T(256)(128)(2,1)} %param.12) | copy-start | bytes 292
  384.1 110.0 %copy-start.16 = (bf16[48,2304]{1,0:T(8,128)(2,1)S(1)}, bf16[48,2304]{1,0:T(8,128)(2,1)}, u32[]{:S(2)}) copy-start(bf16[48,2304]{1,0:T(8,128)(2,1)} %param.10) | copy-start | bytes 663556
  384.1 111.9 %copy-start.25 = (bf16[48]{0:T(256)(128)(2,1)S(1)}, bf16[48]{0:T(256)(128)(2,1)}, u32[]{:S(2)}) copy-start(bf16[48]{0:T(256)(128)(2,1)} %param.9) | copy-start | bytes 292
  388.8 30.0 %collective-permute-start.6 = (bf16[72,768]{1,0:T(8,128)(2,1)}, bf16[72,768]{1,0:T(8,128)(2,1)S(1)}, u32[]{:S(2)}, u32[]{:S(2)}) collective-permute-start(bf16[72,768]{1,0:T(8,128)(2,1)} %reduce-scatter.11.cloned.1.call-done), channel_id=1, source_target_pairs={{0,1},{1,0},{2,3},{3,2},{4,5},{5,4},{6,7},{7,6},{8,9},{9,8},{10,11... | collective-permute-start | bytes 331784 | tf_op jit(solution)/shard_map/ppermute | solution.py:345
  417.2 6.1 %collective-permute-start.5 = (bf16[48,2304]{1,0:T(8,128)(2,1)}, bf16[48,2304]{1,0:T(8,128)(2,1)S(1)}, u32[]{:S(2)}, u32[]{:S(2)}) collective-permute-start(bf16[48,2304]{1,0:T(8,128)(2,1)} %reduce-scatter.9.cloned.1.call-done), channel_id=1, source_target_pairs={{0,1},{1,0},{2,3},{3,2},{4,5},{5,4},{6,7},{7,6},{8,9},{9,8},{10,11... | collective-permute-start | bytes 663560 | tf_op jit(solution)/shard_map/ppermute | solution.py:345
  488.0 6.1 %collective-permute-start.3 = (bf16[48,2304]{1,0:T(8,128)(2,1)}, bf16[48,2304]{1,0:T(8,128)(2,1)S(1)}, u32[]{:S(2)}, u32[]{:S(2)}) collective-permute-start(bf16[48,2304]{1,0:T(8,128)(2,1)} %reduce-scatter.5.cloned.1.call-done), channel_id=1, source_target_pairs={{0,1},{1,0},{2,3},{3,2},{4,5},{5,4},{6,7},{7,6},{8,9},{9,8},{10,11... | collective-permute-start | bytes 663560 | tf_op jit(solution)/shard_map/ppermute | solution.py:345
  (21 other events, 118.6 us)
Sparse Core Ops, SparseCore 0:
  10.7 50.5 all-gather.4
  63.6 37.4 all-gather.6
  103.4 46.1 all-gather.8
  151.6 39.3 all-gather.10
  226.2 57.2 reduce-scatter.6
  287.1 59.1 reduce-scatter.10
  350.2 66.9 reduce-scatter.8
  421.1 66.8 reduce-scatter.4

commit v2 on v1

--- a/solution.py
+++ b/solution.py
@@ -13,6 +13,9 @@
 FF = 1152
 PAIR = 2 * HEAD_DIM
 PAIRS = HEADS // 2
+GROUP = 2
+GROUPS = PAIRS // GROUP
+WIDE = GROUP * PAIR
 
 eps = 1e-05
 rope_base = 160000.0
@@ -78,23 +81,23 @@
         out_ref[...] = u.astype(BF)
 
 
-def project(act, weight, cos_table, sin_table, first, columns, turned, factor):
+def project(act, weight, cos_table, sin_table, first, step, count, turned, factor):
     rows = act.shape[0]
-    wide = 256
+    columns = count * WIDE
     return pl.pallas_call(
-        functools.partial(project_kernel, turned // wide, factor),
-        grid=(columns // wide,),
+        functools.partial(project_kernel, turned, factor),
+        grid=(count,),
         in_specs=[
             pl.BlockSpec((rows, D), lambda c: (0, 0)),
-            pl.BlockSpec((D, wide), lambda c: (0, first // wide + c)),
+            pl.BlockSpec((D, WIDE), lambda c: (0, first + step * c)),
             pl.BlockSpec((rows, PAIR), lambda c: (0, 0)),
             pl.BlockSpec((rows, PAIR), lambda c: (0, 0)),
         ],
-        out_specs=pl.BlockSpec((rows, wide), lambda c: (0, c)),
+        out_specs=pl.BlockSpec((rows, WIDE), lambda c: (0, c)),
         out_shape=jax.ShapeDtypeStruct((rows, columns), BF),
         compiler_params=pltpu.CompilerParams(vmem_limit_bytes=LIMIT),
         cost_estimate=pl.CostEstimate(
-            flops=2 * rows * D * columns, bytes_accessed=4 * rows * D, transcendentals=0
+            flops=rows * D * PAIR, bytes_accessed=rows * PAIR, transcendentals=0
         ),
     )(act, weight, cos_table, sin_table)
 
@@ -150,21 +153,19 @@
 
 def attend_cost(rows, products):
     return pl.CostEstimate(
-        flops=2 * rows * rows * 2 * PAIR * HEADS * products,
-        bytes_accessed=rows * D * 24,
-        transcendentals=rows * rows * HEADS,
-    )
-
-
-def forward(queries, kv, carried):
+        flops=rows * rows * PAIR * products, bytes_accessed=rows * PAIR, transcendentals=0
+    )
+
+
+def forward(group, queries, kv, carried):
     rows = queries.shape[0]
     last = carried is not None
-    wide = jax.ShapeDtypeStruct((rows, D), F32)
-    shapes = [jax.ShapeDtypeStruct((rows, D), BF), wide] if last else [wide, wide, wide]
+    wide = jax.ShapeDtypeStruct((rows, WIDE), F32)
+    shapes = [jax.ShapeDtypeStruct((rows, WIDE), BF), wide] if last else [wide, wide, wide]
     return pl.pallas_call(
         functools.partial(forward_kernel, last, 256),
-        grid=(PAIRS,),
-        in_specs=[pair_spec(rows), pair_spec(rows), pair_spec(rows, PAIRS)]
+        grid=(GROUP,),
+        in_specs=[pair_spec(rows, group * GROUP), pair_spec(rows), pair_spec(rows, GROUP)]
         + [pair_spec(rows)] * (3 if last else 0),
         out_specs=[pair_spec(rows)] * len(shapes),
         out_shape=shapes,
@@ -183,10 +184,10 @@
 def backward_kernel(last, block, *refs):
     if last:
         (q_ref, k_ref, v_ref, g_ref, ctx_ref, lse_ref, cos_ref, sin_ref, dq_in) = refs[:9]
-        dq_ref, dk_ref, dv_ref, qa_ref, ga_ref, sum_ref = refs[9:]
+        dq_ref, dkv_ref, qa_ref, ga_ref, sum_ref = refs[9:]
     else:
         (q_ref, k_ref, v_ref, g_ref, ctx_ref, lse_ref, cos_ref, sin_ref) = refs[:8]
-        dq_ref, dk_ref, dv_ref, qa_ref, ga_ref, sum_ref = refs[8:]
+        dq_ref, dkv_ref, qa_ref, ga_ref, sum_ref = refs[8:]
     count = q_ref.shape[0]
     queries = q_ref[...]
     grads = g_ref[...]
@@ -232,8 +233,8 @@
             else:
                 sum_ref[head] += part
         dk = jnp.where(left_block, dks[0], dks[1])
-        dk_ref[rows, :] = turn(dk, cos_ref[rows, :], -sin_ref[rows, :]).astype(BF)
-        dv_ref[rows, :] = jnp.where(left_block, dvs[0], dvs[1]).astype(BF)
+        dkv_ref[rows, :PAIR] = turn(dk, cos_ref[rows, :], -sin_ref[rows, :]).astype(BF)
+        dkv_ref[rows, PAIR:] = jnp.where(left_block, dvs[0], dvs[1]).astype(BF)
     dq = jnp.where(left, sum_ref[0], sum_ref[1]) * (HEAD_DIM**-0.5)
     if last:
         dq = dq + dq_in[...]
@@ -242,23 +243,26 @@
         dq_ref[...] = dq
 
 
-def backward(queries, kv, grads, ctx, lse, cos_table, sin_table, carried):
+def backward(group, queries, kv, grads, ctx, lse, cos_table, sin_table, carried):
     rows = queries.shape[0]
     last = carried is not None
-    low = jax.ShapeDtypeStruct((rows, D), BF)
+    first = group * GROUP
     table = pl.BlockSpec((rows, PAIR), lambda p: (0, 0))
     args = [queries, kv, kv, grads, ctx, lse, cos_table, sin_table]
-    specs = [pair_spec(rows), pair_spec(rows), pair_spec(rows, PAIRS)]
-    specs += [pair_spec(rows)] * 3 + [table, table]
+    specs = [pair_spec(rows, first), pair_spec(rows), pair_spec(rows, GROUP)]
+    specs += [pair_spec(rows, first), pair_spec(rows), pair_spec(rows), table, table]
     if last:
         args.append(carried)
         specs.append(pair_spec(rows))
     return pl.pallas_call(
         functools.partial(backward_kernel, last, 256),
-        grid=(PAIRS,),
+        grid=(GROUP,),
         in_specs=specs,
-        out_specs=[pair_spec(rows)] * 3,
-        out_shape=[low if last else jax.ShapeDtypeStruct((rows, D), F32), low, low],
+        out_specs=[pair_spec(rows), pl.BlockSpec((rows, 2 * PAIR), lambda p: (0, p))],
+        out_shape=[
+            jax.ShapeDtypeStruct((rows, WIDE), BF if last else F32),
+            jax.ShapeDtypeStruct((rows, 2 * WIDE), BF),
+        ],
         scratch_shapes=[
             pltpu.VMEM((2, rows, PAIR), BF),
             pltpu.VMEM((2, rows, PAIR), BF),
@@ -269,8 +273,21 @@
     )(*args)
 
 
+def after(value, earlier):
+    return lax.optimization_barrier((value, earlier))[0]
+
+
 def gated(gate_part, up_part):
     return jax.nn.gelu(gate_part, approximate=False) * up_part
+
+
+def joined_grads(grad_w_in, grad_w_out, grad_w_down, shard):
+    def by_owner(grad):
+        return grad.astype(BF).reshape(D // shard, -1, D)
+
+    parts = [by_owner(grad_w_in[:, start : start + D]) for start in range(0, 2 * FF, D)]
+    parts += [by_owner(grad_w_out), by_owner(grad_w_down)]
+    return jnp.concatenate(parts, axis=1).reshape(-1, D)
 
 
 def body(tokens, gain_attn, w_qkv, w_out, gain_mlp, w_in, w_down, d_out):
@@ -283,8 +300,8 @@
         [w_qkv, gain_attn[:, None], gain_mlp[:, None], jnp.zeros((shard, PAIR - 2), BF)], axis=1
     )
     packed = lax.all_gather(packed, "dp", axis=0, tiled=True)
-    full_out = lax.all_gather(w_out, "dp", axis=0, tiled=True)
-    full_in = lax.all_gather(w_in, "dp", axis=0, tiled=True)
+    in_out = lax.all_gather(jnp.concatenate([w_in, w_out], axis=1), "dp", axis=0, tiled=True)
+    full_in, full_out = in_out[:, : 2 * FF], in_out[:, 2 * FF :]
     full_down = lax.all_gather(w_down, "dp", axis=0, tiled=True)
     gain_one = packed[:, 3 * D].astype(F32)
     gain_two = packed[:, 3 * D + 1].astype(F32)
@@ -298,11 +315,26 @@
     inputs = tokens.astype(F32)
     normed_one, unit_one, inv_one = normalize_rows(inputs, gain_one)
     act_one = normed_one.astype(BF)
-    kv_here = project(act_one, packed, cos_here, sin_here, D, 2 * D, D, 1.0)
-    kv_there = lax.ppermute(kv_here, "seq", swap)
-    queries = project(act_one, packed, cos_here, sin_here, 0, D, D, HEAD_DIM**-0.5)
-    partial = forward(queries, kv_here, None)
-    ctx, lse = forward(queries, kv_there, partial)
+    kv_here, kv_there = [], []
+    for group in range(GROUPS):
+        kv = project(act_one, packed, cos_here, sin_here, GROUPS + group, GROUPS, 2, 1, 1.0)
+        kv_here.append(kv)
+        kv_there.append(lax.ppermute(kv, "seq", swap))
+    queries = project(
+        act_one, packed, cos_here, sin_here, 0, 1, GROUPS, GROUPS, HEAD_DIM**-0.5
+    )
+    partial, both = [], []
+    last_done = queries
+    for group in range(GROUPS):
+        partial.append(forward(group, after(queries, last_done), kv_here[group], None))
+        last_done = partial[group][1]
+    for group in range(GROUPS):
+        both.append(
+            forward(group, after(queries, last_done), kv_there[group], partial[group])
+        )
+        last_done = both[group][1]
+    ctx_parts, lse_parts = [pair[0] for pair in both], [pair[1] for pair in both]
+    ctx = jnp.concatenate(ctx_parts, axis=1)
 
     attended = jnp.dot(ctx, full_out, preferred_element_type=F32)
     hidden = inputs + attended
@@ -325,29 +357,49 @@
     grad_w_out = dot(ctx, grad_hidden_low, 0, 0)
     grad_ctx = dot(grad_hidden_low, full_out, 1, 1).astype(BF)
 
-    dq_part, dk_far, dv_far = backward(
-        queries, kv_there, grad_ctx, ctx, lse, cos_there, sin_there, None
-    )
-    dk_got = lax.ppermute(dk_far, "seq", swap)
-    dv_got = lax.ppermute(dv_far, "seq", swap)
-    dq, dk, dv = backward(queries, kv_here, grad_ctx, ctx, lse, cos_here, sin_here, dq_part)
-    dk = (dk.astype(F32) + dk_got.astype(F32)).astype(BF)
-    dv = (dv.astype(F32) + dv_got.astype(F32)).astype(BF)
-    grad_proj = jnp.concatenate([dq, dk, dv], axis=1)
+    joined = joined_grads(grad_w_in, grad_w_out, grad_w_down, shard)
+    joined = lax.psum_scatter(joined, "dp", scatter_dimension=0, tiled=True)
+    dq_parts, dkv_got = [], []
+    last_done = grad_ctx
+    for group in range(GROUPS):
+        dq_part, dkv_far = backward(
+            group, after(queries, last_done), kv_there[group], grad_ctx, ctx_parts[group], lse_parts[group],
+            cos_there, sin_there, None,
+        )
+        dq_parts.append(dq_part)
+        last_done = dq_part
+        dkv_got.append(lax.ppermute(dkv_far, "seq", swap))
+    dqs, dks, dvs = [], [], []
+    for group in range(GROUPS):
+        last_done = (last_done, dkv_got[group] if group + 1 < GROUPS else joined)
+        dq, dkv = backward(
+            group, after(queries, last_done), kv_here[group], grad_ctx, ctx_parts[group], lse_parts[group],
+            cos_here, sin_here, dq_parts[group],
+        )
+        last_done = dq
+        dkv = (dkv.astype(F32) + dkv_got[group].astype(F32)).astype(BF)
+        dqs.append(dq)
+        for start in range(0, 2 * WIDE, 2 * PAIR):
+            dks.append(dkv[:, start : start + PAIR])
+            dvs.append(dkv[:, start + PAIR : start + 2 * PAIR])
+    grad_proj = jnp.concatenate(dqs + dks + dvs, axis=1)
 
     grad_w_qkv = dot(act_one, grad_proj, 0, 0)
     full_qkv = packed[:, : 3 * D]
     grad_norm_one = dot(grad_proj, full_qkv, 1, 1)
     grad_tokens = grad_hidden + normalize_back(grad_norm_one, gain_one, unit_one, inv_one)
 
-    def owned(grad):
-        part = lax.psum_scatter(grad.astype(BF), "dp", scatter_dimension=0, tiled=True)
+    def owned(part):
         other = lax.ppermute(part, "seq", swap)
         return part.astype(F32) + other.astype(F32)
 
-    own_down, own_in, own_out, own_qkv = (
-        owned(grad_w_down), owned(grad_w_in), owned(grad_w_out), owned(grad_w_qkv)
-    )
+    grad_w_qkv = after(grad_w_qkv.astype(BF), joined)
+    part_qkv = lax.psum_scatter(grad_w_qkv, "dp", scatter_dimension=0, tiled=True)
+    own_joined = owned(joined)
+    own_in = jnp.concatenate([own_joined[k * shard : (k + 1) * shard] for k in range(3)], axis=1)
+    own_out = own_joined[3 * shard : 4 * shard]
+    own_down = own_joined[4 * shard :]
+    own_qkv = owned(part_qkv)
     own_gain_one = jnp.sum(own_qkv * w_qkv.astype(F32), axis=1) / gain_attn.astype(F32)
     own_gain_two = jnp.sum(own_in * w_in.astype(F32), axis=1) / gain_mlp.astype(F32)
     return (

time: 508 us -> 442 us (0.87)
  waiting for transfers between devices: 198 us -> 92.3 us
  Pallas kernels: 161 us -> 189 us
  local copies, waits for them, and re-layouts: 12.2 us -> 35.4 us
  matrix products: 74.7 us -> 67.5 us
  other arithmetic: 33.7 us -> 27.5 us
    ppermute x3 -> x6, waiting for transfers between devices: 58 us -> 0.02 us  [the longest x3 0.01 us: body(): dkv_got.append(lax.ppermute(dkv_far, 'seq', swap))]
    reduce_scatter x4 -> x2, waiting for transfers between devices: 89.9 us -> 47 us  [the longest x1 47 us: body(): lax.psum_scatter(grad_w_qkv, 'dp', scatter_dimension=0, tiled=True)]
    pallas_call x6 -> x16, Pallas kernels: 161 us -> 189 us  [the longest x6 100 us: backward(): pl.pallas_call(functools.partial(backward_kernel, last, 256), grid=(GROUP...]
    unnamed x60 -> x94, local copies, waits for them, and re-layouts: 8.93 us -> 26.4 us
  transfers between devices with their start and end apart: 15 -> 13, of which waited for: 7 -> 3; matrix products, arithmetic and copies ran while one was open for 15% -> 14% of each run, Pallas kernels for 32% -> 43%
where the time goes in v2:
time: 442 us; the launch traced here: 436 us
  Pallas kernels  189 us (43%)
  waiting for transfers between devices  92.3 us (21%)
  matrix products  67.5 us (15%)
  local copies, waits for them, and re-layouts  35.4 us (8%)
  other arithmetic  27.5 us (6%)
  between operations  14.8 us (3%)
  starting transfers between devices  9.77 us (2%)
    pallas_call x6, Pallas kernels, backward(): pl.pallas_call(functools.partial(backward_kernel, last, 256), grid=(GROUP...  100 us
    pallas_call x6, Pallas kernels, forward(): pl.pallas_call(functools.partial(forward_kernel, last, 256), grid=(GROUP,...  68.3 us
    dot_general x8, matrix products, dot(): lax.dot_general(a, b, (((a_dim,), (b_dim,)), ((), ())), preferred_element...  51.3 us
    reduce_scatter x1, waiting for transfers between devices, body(): lax.psum_scatter(grad_w_qkv, 'dp', scatter_dimension=0, tiled=True)  47 us
    all_gather x1, waiting for transfers between devices, body(): packed = lax.all_gather(packed, 'dp', axis=0, tiled=True)  41 us
    unnamed x94, local copies, waits for them, and re-layouts  26.4 us
    pallas_call x4, Pallas kernels, project(): pl.pallas_call(functools.partial(project_kernel, turned, factor), grid=(c...  20.6 us
  transfers between devices with their start and end apart: 13, of which 3 were waited for; matrix products, arithmetic and copies ran while one was open for 14% of the time, Pallas kernels for 43%

profile of v2, /device:TPU:0, one launch (start us, length us, event | category | flops | bytes accessed | tf_op | source)
XLA Modules:
  0.0 436.2 jit_solution(16616643500420470518)
XLA Ops:
  12.5 5.0 %fusion.29 = (f32[1024,32]{1,0:T(8,128)}, f32[1024,32]{1,0:T(8,128)}, f32[1024,32]{1,0:T(8,128)}, f32[1024,32]{1,0:T(8,128)S(1)}, f32[1024,32]{1,0:T(8,128)S(1)}, /*index=5*/f32[1024,32]{1,0:T(8,128)S(1)}) fusion(f32[32]{0:T(128)S(1)} %multiply_power_fusion, f32[1024]{0:T(1024)S(1)} %add_convert_fusion.5, f32[1024]{0:T(1024)S(1)} %add_convert_fusion.6), kind=kLoop, calls=%fused_computation.90 | loop fusion | flops 131072 | bytes 794752 | tf_op jit(solution)/shard_map/neg | solution.py:51
  20.3 41.0 %all-gather.4.cloned.1.call-done.w_ref = bf16[768,2432]{1,0:T(8,128)(2,1)} async-done(((bf16[48,2432]{1,0:T(8,128)(2,1)}), bf16[768,2432]{1,0:T(8,128)(2,1)}) %all-gather.4.cloned.1.call-update) | async-done | bytes 3735568 | tf_op jit(solution)/shard_map/all_gather | solution.py:302
  71.0 4.7 %shard_map.146.refs_1_.refs_2_ = bf16[1024,512]{1,0:T(8,128)(2,1)} custom-call(bf16[1024,768]{1,0:T(8,128)(2,1)} %fusion.14.act_ref, bf16[768,2432]{1,0:T(8,128)(2,1)} %all-gather.4.cloned.1.call-done.w_ref, f32[1024,128]{1,0:T(8,128)} %get-tuple-element.123.cos_ref.refs_6_, f32[1024,128]{1,0:T(8,128)} %get-tuple-element.124.sin_ref.refs_7_), custom_call_target="tpu_custom_call" | custom-call | flops 100663296 | bytes 131072 | tf_op jit(solution)/shard_map/pallas_call | solution.py:87
  82.6 6.8 %shard_map.143.refs_0_ = bf16[1024,768]{1,0:T(8,128)(2,1)} custom-call(bf16[1024,768]{1,0:T(8,128)(2,1)} %fusion.14.act_ref, bf16[768,2432]{1,0:T(8,128)(2,1)} %all-gather.4.cloned.1.call-done.w_ref, f32[1024,128]{1,0:T(8,128)} %get-tuple-element.123.cos_ref.refs_6_, f32[1024,128]{1,0:T(8,128)} %get-tuple-element.124.sin_ref.refs_7_), custom_call_target="tpu_custom_call" | custom-call | flops 100663296 | bytes 131072 | tf_op jit(solution)/shard_map/pallas_call | solution.py:87
  89.3 10.0 %shard_map.145 = (f32[1024,256]{1,0:T(8,128)}, f32[1024,256]{1,0:T(8,128)}, f32[1024,256]{1,0:T(8,128)}) custom-call(bf16[1024,768]{1,0:T(8,128)(2,1)} %shard_map.143.refs_0_, bf16[1024,512]{1,0:T(8,128)(2,1)} %shard_map.144.refs_1_.refs_2_, bf16[1024,512]{1,0:T(8,128)(2,1)} %shard_map.144.refs_1_.refs_2_), custom_call_target="tpu_custom_call" | custom-call | flops 268435456 | bytes 131072 | tf_op jit(solution)/shard_map/pallas_call | solution.py:165
  99.3 10.0 %shard_map.147 = (f32[1024,256]{1,0:T(8,128)}, f32[1024,256]{1,0:T(8,128)}, f32[1024,256]{1,0:T(8,128)}) custom-call(bf16[1024,768]{1,0:T(8,128)(2,1)} %shard_map.143.refs_0_, bf16[1024,512]{1,0:T(8,128)(2,1)} %shard_map.146.refs_1_.refs_2_, bf16[1024,512]{1,0:T(8,128)(2,1)} %shard_map.146.refs_1_.refs_2_), custom_call_target="tpu_custom_call" | custom-call | flops 268435456 | bytes 131072 | tf_op jit(solution)/shard_map/pallas_call | solution.py:165
  109.3 10.2 %shard_map.149 = (f32[1024,256]{1,0:T(8,128)}, f32[1024,256]{1,0:T(8,128)}, f32[1024,256]{1,0:T(8,128)}) custom-call(bf16[1024,768]{1,0:T(8,128)(2,1)} %shard_map.143.refs_0_, bf16[1024,512]{1,0:T(8,128)(2,1)} %shard_map.148.refs_1_.refs_2_, bf16[1024,512]{1,0:T(8,128)(2,1)} %shard_map.148.refs_1_.refs_2_), custom_call_target="tpu_custom_call" | custom-call | flops 268435456 | bytes 131072 | tf_op jit(solution)/shard_map/pallas_call | solution.py:165
  119.5 12.5 %shard_map.150 = (bf16[1024,256]{1,0:T(8,128)(2,1)}, f32[1024,256]{1,0:T(8,128)}) custom-call(bf16[1024,768]{1,0:T(8,128)(2,1)} %shard_map.143.refs_0_, bf16[1024,512]{1,0:T(8,128)(2,1)} %collective-permute-done.refs_1_.refs_2_, bf16[1024,512]{1,0:T(8,128)(2,1)} %collective-permute-done.refs_1_.refs_2_, f32[1024,256]{1,0:T(8,128)} %get-tuple-element.55.refs_3_, ...), custom_call_target="tpu_custom_call" | custom-call | flops 268435456 | bytes 131072 | tf_op jit(solution)/shard_map/pallas_call | solution.py:165
  132.0 13.0 %shard_map.151 = (bf16[1024,256]{1,0:T(8,128)(2,1)}, f32[1024,256]{1,0:T(8,128)}) custom-call(bf16[1024,768]{1,0:T(8,128)(2,1)} %shard_map.143.refs_0_, bf16[1024,512]{1,0:T(8,128)(2,1)} %collective-permute-done.1.refs_1_.refs_2_, bf16[1024,512]{1,0:T(8,128)(2,1)} %collective-permute-done.1.refs_1_.refs_2_, f32[1024,256]{1,0:T(8,128)} %get-tuple-element.60.refs_3_, ...), custom_call_target="tpu_custom_call" | custom-call | flops 268435456 | bytes 131072 | tf_op jit(solution)/shard_map/pallas_call | solution.py:165
  146.0 12.6 %shard_map.152 = (bf16[1024,256]{1,0:T(8,128)(2,1)}, f32[1024,256]{1,0:T(8,128)}) custom-call(bf16[1024,768]{1,0:T(8,128)(2,1)} %shard_map.143.refs_0_, bf16[1024,512]{1,0:T(8,128)(2,1)} %copy-done.3, bf16[1024,512]{1,0:T(8,128)(2,1)} %copy-done.3, f32[1024,256]{1,0:T(8,128)} %get-tuple-element.65.refs_3_, f32[1024,256]{1,0:T(8,128)} %get-tuple-element.53.refs_4_, ...), custom_call_target="tpu_custom_call" | custom-call | flops 268435456 | bytes 131072 | tf_op jit(solution)/shard_map/pallas_call | solution.py:165
  167.4 6.7 %fusion.22 = f32[1024,2304]{1,0:T(8,128)} fusion(bf16[768,3072]{1,0:T(8,128)(2,1)S(1)} %copy-done.32, f32[1024,768]{1,0:T(8,128)S(1)} %get-tuple-element.119, f32[768]{0:T(1024)S(1)} %get-tuple-element.88, f32[1024]{0:T(1024)S(1)} %add_rsqrt_fusion, f32[1024]{0:T(1024)S(1)} %broadcast_multiply_fusion.4), kind=kOutput, calls=%fused_computation.47 | convolution fusion | flops 3627024384 | bytes 16134144 | tf_op jit(solution)/shard_map/dot_general | solution.py:343
  174.1 16.1 %add_convert_fusion = (bf16[1024,1152]{1,0:T(8,128)(2,1)}, f32[1024,1152]{1,0:T(8,128)S(1)}, f32[1024,1152]{1,0:T(8,128)S(1)}) fusion(f32[1024,2304]{1,0:T(8,128)} %fusion.22, bf16[1024,768]{1,0:T(8,128)(2,1)S(1)} %copy-done.16, bf16[1152,768]{1,0:T(8,128)(2,1)} %all-gather.8.cloned.1.call-done), kind=kOutput, calls=%fused_computation.9 | convolution fusion | flops 1898053632 | bytes 24576000 | tf_op jit(solution)/shard_map/dot_general | solution.py:66
  199.5 5.9 %multiply_reduce_fusion.3 = (f32[1024]{0:T(1024)S(1)}, f32[1024]{0:T(1024)S(1)}, f32[1024,768]{1,0:T(8,128)S(1)}) fusion(f32[768]{0:T(1024)S(1)} %get-tuple-element.88, f32[1024]{0:T(1024)S(1)} %add_rsqrt_fusion, f32[1024,768]{1,0:T(8,128)S(1)} %copy-done.5, f32[1024]{0:T(1024)S(1)} %broadcast_multiply_fusion.4, bf16[768,3072]{1,0:T(8,128)(2,1)S(1)} %bitcast.27, ...), kind=kOutput, calls=%fused_computation.51 | convolution fusion | flops 3638032384 | bytes 14569472 | tf_op jit(solution)/shard_map/dot_general | solution.py:66
  220.1 4.9 %convolution_convert_fusion.3.refs_3_ = bf16[1024,768]{1,0:T(8,128)(2,1)} fusion(bf16[768,3072]{1,0:T(8,128)(2,1)} %all-gather.6.cloned.1.call-done, f32[1024,768]{1,0:T(8,128)} %copy-done.6), kind=kOutput, calls=%fused_computation.55 | convolution fusion | flops 1209532416 | bytes 5898240 | tf_op jit(solution)/shard_map/dot_general | solution.py:66
  225.0 16.3 %shard_map.153 = (f32[1024,256]{1,0:T(8,128)}, bf16[1024,512]{1,0:T(8,128)(2,1)}) custom-call(bf16[1024,768]{1,0:T(8,128)(2,1)} %shard_map.143.refs_0_, bf16[1024,512]{1,0:T(8,128)(2,1)} %collective-permute-done.refs_1_.refs_2_, bf16[1024,512]{1,0:T(8,128)(2,1)} %collective-permute-done.refs_1_.refs_2_, bf16[1024,768]{1,0:T(8,128)(2,1)} %convolution_convert_fusion.3.refs_3_, ...), custom_call_target="tpu_custom_call" | custom-call | flops 671088640 | bytes 131072 | tf_op jit(solution)/shard_map/pallas_call | solution.py:257
  242.2 16.6 %shard_map.154 = (f32[1024,256]{1,0:T(8,128)}, bf16[1024,512]{1,0:T(8,128)(2,1)}) custom-call(bf16[1024,768]{1,0:T(8,128)(2,1)} %shard_map.143.refs_0_, bf16[1024,512]{1,0:T(8,128)(2,1)} %collective-permute-done.1.refs_1_.refs_2_, bf16[1024,512]{1,0:T(8,128)(2,1)} %collective-permute-done.1.refs_1_.refs_2_, ...), custom_call_target="tpu_custom_call" | custom-call | flops 671088640 | bytes 131072 | tf_op jit(solution)/shard_map/pallas_call | solution.py:257
  260.0 16.3 %shard_map.155 = (f32[1024,256]{1,0:T(8,128)}, bf16[1024,512]{1,0:T(8,128)(2,1)}) custom-call(bf16[1024,768]{1,0:T(8,128)(2,1)} %shard_map.143.refs_0_, bf16[1024,512]{1,0:T(8,128)(2,1)} %copy-done.3, bf16[1024,512]{1,0:T(8,128)(2,1)} %copy-done.3, bf16[1024,768]{1,0:T(8,128)(2,1)} %convolution_convert_fusion.3.refs_3_, ...), custom_call_target="tpu_custom_call" | custom-call | flops 671088640 | bytes 131072 | tf_op jit(solution)/shard_map/pallas_call | solution.py:257
  277.1 16.8 %shard_map.156 = (bf16[1024,256]{1,0:T(8,128)(2,1)}, bf16[1024,512]{1,0:T(8,128)(2,1)}) custom-call(bf16[1024,768]{1,0:T(8,128)(2,1)} %shard_map.143.refs_0_, bf16[1024,512]{1,0:T(8,128)(2,1)} %shard_map.144.refs_1_.refs_2_, bf16[1024,512]{1,0:T(8,128)(2,1)} %shard_map.144.refs_1_.refs_2_, bf16[1024,768]{1,0:T(8,128)(2,1)} %convolution_convert_fusion.3.refs_3_, ...), custom_call_target="tpu_custom_call" | custom-call | flops 671088640 | bytes 131072 | tf_op jit(solution)/shard_map/pallas_call | solution.py:257
  294.0 17.1 %shard_map.157 = (bf16[1024,256]{1,0:T(8,128)(2,1)}, bf16[1024,512]{1,0:T(8,128)(2,1)}) custom-call(bf16[1024,768]{1,0:T(8,128)(2,1)} %shard_map.143.refs_0_, bf16[1024,512]{1,0:T(8,128)(2,1)} %shard_map.146.refs_1_.refs_2_, bf16[1024,512]{1,0:T(8,128)(2,1)} %shard_map.146.refs_1_.refs_2_, bf16[1024,768]{1,0:T(8,128)(2,1)} %convolution_convert_fusion.3.refs_3_, ...), custom_call_target="tpu_custom_call" | custom-call | flops 671088640 | bytes 131072 | tf_op jit(solution)/shard_map/pallas_call | solution.py:257
  315.7 16.9 %shard_map.158 = (bf16[1024,256]{1,0:T(8,128)(2,1)}, bf16[1024,512]{1,0:T(8,128)(2,1)}) custom-call(bf16[1024,768]{1,0:T(8,128)(2,1)} %shard_map.143.refs_0_, bf16[1024,512]{1,0:T(8,128)(2,1)} %shard_map.148.refs_1_.refs_2_, bf16[1024,512]{1,0:T(8,128)(2,1)} %shard_map.148.refs_1_.refs_2_, bf16[1024,768]{1,0:T(8,128)(2,1)} %convolution_convert_fusion.3.refs_3_, ...), custom_call_target="tpu_custom_call" | custom-call | flops 671088640 | bytes 131072 | tf_op jit(solution)/shard_map/pallas_call | solution.py:257
  345.6 7.6 %convolution_convert_fusion = bf16[768,2304]{1,0:T(8,128)(2,1)} fusion(bf16[1024,768]{1,0:T(8,128)(2,1)S(1)} %copy-done.1, bf16[1024,2304]{1,0:T(8,128)(2,1)} %slice_dynamic-update-slice_fusion), kind=kOutput, calls=%fused_computation.1 | convolution fusion | flops 3625648128 | bytes 9830400 | tf_op jit(solution)/shard_map/dot_general | solution.py:66
  354.7 6.1 %add_convert_fusion.1 = bf16[1024,768]{1,0:T(8,128)(2,1)} fusion(f32[1024,768]{1,0:T(8,128)} %copy-done.4, bf16[1024,1152]{1,0:T(8,128)(2,1)} %copy-done.12, bf16[1152,768]{1,0:T(8,128)(2,1)S(1)} %copy-done.33), kind=kOutput, calls=%fused_computation.42 | convolution fusion | flops 1813512192 | bytes 8847360 | tf_op jit(solution)/shard_map/dot_general | solution.py:346
  362.0 6.6 %multiply_reduce_fusion.2 = (f32[1024]{0:T(1024)S(1)}, f32[1024]{0:T(1024)S(1)}, f32[1024,768]{1,0:T(8,128)S(1)}) fusion(f32[768]{0:T(1024)S(1)} %copy-done.27, f32[1024]{0:T(1024)S(1)} %copy-done.29, f32[1024]{0:T(1024)S(1)} %copy-done.25, bf16[1024,768]{1,0:T(8,128)(2,1)S(1)} %copy-done.2, bf16[1024,2304]{1,0:T(8,128)(2,1)} %slice_dynamic-update-slice_fusion, ...), kind=kOutput, calls=%fused_computation.50 | convolution fusion | flops 3629381632 | bytes 12996608 | tf_op jit(solution)/shard_map/dot_general | solution.py:66
  373.5 47.0 %reduce-scatter.5.cloned.1.call-done = bf16[48,2304]{1,0:T(8,128)(2,1)} async-done(((bf16[768,2304]{1,0:T(8,128)(2,1)}), bf16[48,2304]{1,0:T(8,128)(2,1)}) %reduce-scatter.5.cloned.1.call-update) | async-done | bytes 221200 | tf_op jit(solution)/shard_map/reduce_scatter | solution.py:397
  (170 shorter events, 94.7 us)
Async XLA Ops:
  7.2 54.1 %all-gather.4.cloned.1.call-start = ((), (), s32[]{:S(2)}) async-start(), calls=%async_computation.2 | async-start | bytes 3969024 | tf_op jit(solution)/shard_map/all_gather | solution.py:302
  10.5 151.8 %all-gather.6.cloned.1.call-start = ((), (), s32[]{:S(2)}) async-start(), calls=%async_computation.3 | async-start | bytes 5013504 | tf_op jit(solution)/shard_map/all_gather | solution.py:303
  12.4 161.8 %all-gather.8.cloned.1.call-start = ((), (), s32[]{:S(2)}) async-start(), calls=%async_computation.4 | async-start | bytes 1880064 | tf_op jit(solution)/shard_map/all_gather | solution.py:305
  19.7 49.8 %copy-start.24 = (f32[1024]{0:T(1024)}, f32[1024]{0:T(1024)S(1)}, u32[]{:S(2)}) copy-start(f32[1024]{0:T(1024)S(1)} %broadcast_multiply_fusion.5) | copy-start | bytes 12292
  20.3 49.2 %copy-start.28 = (f32[1024]{0:T(1024)}, f32[1024]{0:T(1024)S(1)}, u32[]{:S(2)}) copy-start(f32[1024]{0:T(1024)S(1)} %add_rsqrt_fusion.1) | copy-start | bytes 12292
  69.5 50.0 %collective-permute-start = (bf16[1024,512]{1,0:T(8,128)(2,1)}, bf16[1024,512]{1,0:T(8,128)(2,1)}, u32[]{:S(2)}, u32[]{:S(2)}) collective-permute-start(bf16[1024,512]{1,0:T(8,128)(2,1)} %shard_map.144.refs_1_.refs_2_), channel_id=1, source_target_pairs={{0,1},{1,0},{2,3},{3,2},{4,5},{5,4},{6,7},{7,6},{8,9},{9,8},{10,11... | collective-permute-start | bytes 3145736 | tf_op jit(solution)/shard_map/ppermute | solution.py:322
  75.7 56.3 %collective-permute-start.1 = (bf16[1024,512]{1,0:T(8,128)(2,1)}, bf16[1024,512]{1,0:T(8,128)(2,1)}, u32[]{:S(2)}, u32[]{:S(2)}) collective-permute-start(bf16[1024,512]{1,0:T(8,128)(2,1)} %shard_map.146.refs_1_.refs_2_), channel_id=1, source_target_pairs={{0,1},{1,0},{2,3},{3,2},{4,5},{5,4},{6,7},{7,6},{8,9},{9,8},{10,11... | collective-permute-start | bytes 3145736 | tf_op jit(solution)/shard_map/ppermute | solution.py:322
  80.8 64.2 %collective-permute-start.2 = (bf16[1024,512]{1,0:T(8,128)(2,1)}, bf16[1024,512]{1,0:T(8,128)(2,1)S(1)}, u32[]{:S(2)}, u32[]{:S(2)}) collective-permute-start(bf16[1024,512]{1,0:T(8,128)(2,1)} %shard_map.148.refs_1_.refs_2_), channel_id=1, source_target_pairs={{0,1},{1,0},{2,3},{3,2},{4,5},{5,4},{6,7},{7,6},{8,9},{9,8},{10,11... | collective-permute-start | bytes 3145736 | tf_op jit(solution)/shard_map/ppermute | solution.py:322
  82.3 233.4 %reduce-scatter.3.cloned.1.call-start = ((), (), s32[]{:S(2)}) async-start(), calls=%async_computation.5 | async-start | bytes 6893568 | tf_op jit(solution)/shard_map/reduce_scatter | solution.py:361
  145.0 13.6 %copy-start.10 = (bf16[1024,256]{1,0:T(8,128)(2,1)S(1)}, bf16[1024,256]{1,0:T(8,128)(2,1)}, u32[]{:S(2)}) copy-start(bf16[1024,256]{1,0:T(8,128)(2,1)} %get-tuple-element.57.refs_4_) | copy-start | bytes 1572868
  146.0 13.5 %copy-start.9 = (bf16[1024,256]{1,0:T(8,128)(2,1)S(1)}, bf16[1024,256]{1,0:T(8,128)(2,1)}, u32[]{:S(2)}) copy-start(bf16[1024,256]{1,0:T(8,128)(2,1)} %get-tuple-element.62.refs_4_) | copy-start | bytes 1572868
  174.1 16.1 %copy-start.8 = (f32[1024,2304]{1,0:T(8,128)S(1)}, f32[1024,2304]{1,0:T(8,128)}, u32[]{:S(2)}) copy-start(f32[1024,2304]{1,0:T(8,128)} %fusion.22) | copy-start | bytes 28311556
  216.9 203.6 %reduce-scatter.5.cloned.1.call-start = ((), (), s32[]{:S(2)}) async-start(), calls=%async_computation.6 | async-start | bytes 3760128 | tf_op jit(solution)/shard_map/reduce_scatter | solution.py:397
  241.3 35.8 %collective-permute-start.3 = (bf16[1024,512]{1,0:T(8,128)(2,1)}, bf16[1024,512]{1,0:T(8,128)(2,1)S(1)}, u32[]{:S(2)}, u32[]{:S(2)}) collective-permute-start(bf16[1024,512]{1,0:T(8,128)(2,1)} %get-tuple-element.75), channel_id=1, source_target_pairs={{0,1},{1,0},{2,3},{3,2},{4,5},{5,4},{6,7},{7,6},{8,9},{9,8},{10,11... | collective-permute-start | bytes 3145736 | tf_op jit(solution)/shard_map/ppermute | solution.py:371
  258.8 35.2 %collective-permute-start.4 = (bf16[1024,512]{1,0:T(8,128)(2,1)}, bf16[1024,512]{1,0:T(8,128)(2,1)S(1)}, u32[]{:S(2)}, u32[]{:S(2)}) collective-permute-start(bf16[1024,512]{1,0:T(8,128)(2,1)} %get-tuple-element.78), channel_id=1, source_target_pairs={{0,1},{1,0},{2,3},{3,2},{4,5},{5,4},{6,7},{7,6},{8,9},{9,8},{10,11... | collective-permute-start | bytes 3145736 | tf_op jit(solution)/shard_map/ppermute | solution.py:371
  276.3 61.4 %collective-permute-start.5 = (bf16[1024,512]{1,0:T(8,128)(2,1)}, bf16[1024,512]{1,0:T(8,128)(2,1)}, u32[]{:S(2)}, u32[]{:S(2)}) collective-permute-start(bf16[1024,512]{1,0:T(8,128)(2,1)} %get-tuple-element.86), channel_id=1, source_target_pairs={{0,1},{1,0},{2,3},{3,2},{4,5},{5,4},{6,7},{7,6},{8,9},{9,8},{10,11... | collective-permute-start | bytes 3145736 | tf_op jit(solution)/shard_map/ppermute | solution.py:371
  294.0 17.1 %copy-start.22 = (bf16[1024,256]{1,0:T(8,128)(2,1)S(1)}, bf16[1024,256]{1,0:T(8,128)(2,1)}, u32[]{:S(2)}) copy-start(bf16[1024,256]{1,0:T(8,128)(2,1)} %get-tuple-element.77) | copy-start | bytes 1572868
  294.0 20.1 %copy-start.18 = (bf16[1024,512]{1,0:T(8,128)(2,1)S(1)}, bf16[1024,512]{1,0:T(8,128)(2,1)}, u32[]{:S(2)}) copy-start(bf16[1024,512]{1,0:T(8,128)(2,1)} %get-tuple-element.83) | copy-start | bytes 3145732
  315.7 18.9 %copy-start.11 = (bf16[1024,512]{1,0:T(8,128)(2,1)S(1)}, bf16[1024,512]{1,0:T(8,128)(2,1)}, u32[]{:S(2)}) copy-start(bf16[1024,512]{1,0:T(8,128)(2,1)} %add_convert_fusion.4) | copy-start | bytes 3145732
  360.8 10.3 %collective-permute-start.7 = (bf16[264,768]{1,0:T(8,128)(2,1)S(1)}, bf16[264,768]{1,0:T(8,128)(2,1)S(1)}, u32[]{:S(2)}, u32[]{:S(2)}) collective-permute-start(bf16[264,768]{1,0:T(8,128)(2,1)S(1)} %copy-done.23), channel_id=1, source_target_pairs={{0,1},{1,0},{2,3},{3,2},{4,5},{5,4},{6,7},{7,6},{8,9},{9,8},{10,11... | collective-permute-start | bytes 1216520 | tf_op jit(solution)/shard_map/ppermute | solution.py:393
  371.1 51.0 %copy-start.30 = (bf16[48]{0:T(256)(128)(2,1)S(1)}, bf16[48]{0:T(256)(128)(2,1)}, u32[]{:S(2)}) copy-start(bf16[48]{0:T(256)(128)(2,1)} %param.12) | copy-start | bytes 292
  371.1 55.6 %copy-start.21 = (bf16[48,2304]{1,0:T(8,128)(2,1)S(1)}, bf16[48,2304]{1,0:T(8,128)(2,1)}, u32[]{:S(2)}) copy-start(bf16[48,2304]{1,0:T(8,128)(2,1)} %param.10) | copy-start | bytes 663556
  371.1 57.5 %copy-start.31 = (bf16[48]{0:T(256)(128)(2,1)S(1)}, bf16[48]{0:T(256)(128)(2,1)}, u32[]{:S(2)}) copy-start(bf16[48]{0:T(256)(128)(2,1)} %param.9) | copy-start | bytes 292
  420.5 6.1 %collective-permute-start.6 = (bf16[48,2304]{1,0:T(8,128)(2,1)}, bf16[48,2304]{1,0:T(8,128)(2,1)S(1)}, u32[]{:S(2)}, u32[]{:S(2)}) collective-permute-start(bf16[48,2304]{1,0:T(8,128)(2,1)} %reduce-scatter.5.cloned.1.call-done), channel_id=1, source_target_pairs={{0,1},{1,0},{2,3},{3,2},{4,5},{5,4},{6,7},{7,6},{8,9},{9,8},{10,11... | collective-permute-start | bytes 663560 | tf_op jit(solution)/shard_map/ppermute | solution.py:393
  (26 other events, 117.6 us)
Sparse Core Ops, SparseCore 0:
  10.7 50.5 all-gather.3
  64.2 52.4 all-gather.5
  118.8 38.8 all-gather.7
  217.0 85.2 reduce-scatter.2
  353.3 67.1 reduce-scatter.4

commit v3 on v2

--- a/solution.py
+++ b/solution.py
@@ -13,7 +13,7 @@
 FF = 1152
 PAIR = 2 * HEAD_DIM
 PAIRS = HEADS // 2
-GROUP = 2
+GROUP = 3
 GROUPS = PAIRS // GROUP
 WIDE = GROUP * PAIR
 
@@ -113,7 +113,8 @@
 
 def forward_kernel(last, block, *refs):
     if last:
-        q_ref, k_ref, v_ref, o_in, m_in, l_in, ctx_ref, lse_ref = refs
+        q_ref, k_ref, v_ref, o_in, m_in, l_in = refs[:6]
+        ctx_ref, lse_ref = refs[-2:]
     else:
         q_ref, k_ref, v_ref, o_ref, m_ref, l_ref = refs
     keys = k_ref[...]
@@ -157,21 +158,32 @@
     )
 
 
-def forward(group, queries, kv, carried):
+def forward(group, queries, kv, carried, context=None):
     rows = queries.shape[0]
     last = carried is not None
     wide = jax.ShapeDtypeStruct((rows, WIDE), F32)
-    shapes = [jax.ShapeDtypeStruct((rows, WIDE), BF), wide] if last else [wide, wide, wide]
+    shapes = [jax.ShapeDtypeStruct((rows, D), BF), wide] if last else [wide, wide, wide]
+    outs = [pair_spec(rows)] * len(shapes)
+    args, specs, aliases = [queries, kv, kv], [], {}
+    if last:
+        outs[0] = pair_spec(rows, group * GROUP)
+        args += list(carried)
+        if context is not None:
+            aliases = {len(args): 0}
+            args.append(context)
+            specs = [pl.BlockSpec(memory_space=pl.ANY)]
     return pl.pallas_call(
         functools.partial(forward_kernel, last, 256),
         grid=(GROUP,),
         in_specs=[pair_spec(rows, group * GROUP), pair_spec(rows), pair_spec(rows, GROUP)]
-        + [pair_spec(rows)] * (3 if last else 0),
-        out_specs=[pair_spec(rows)] * len(shapes),
+        + [pair_spec(rows)] * (3 if last else 0)
+        + specs,
+        out_specs=outs,
         out_shape=shapes,
+        input_output_aliases=aliases,
         compiler_params=pltpu.CompilerParams(vmem_limit_bytes=LIMIT),
         cost_estimate=attend_cost(rows, 2),
-    )(queries, kv, kv, *(carried or ()))
+    )(*args)
 
 
 def split_three(values_in):
@@ -250,7 +262,7 @@
     table = pl.BlockSpec((rows, PAIR), lambda p: (0, 0))
     args = [queries, kv, kv, grads, ctx, lse, cos_table, sin_table]
     specs = [pair_spec(rows, first), pair_spec(rows), pair_spec(rows, GROUP)]
-    specs += [pair_spec(rows, first), pair_spec(rows), pair_spec(rows), table, table]
+    specs += [pair_spec(rows, first), pair_spec(rows, first), pair_spec(rows), table, table]
     if last:
         args.append(carried)
         specs.append(pair_spec(rows))
@@ -273,6 +285,34 @@
     )(*args)
 
 
+def join_kernel(*refs):
+    out_ref = refs[-1]
+    for group in range(GROUPS):
+        dq_ref, own_ref, got_ref = refs[group : 3 * GROUPS : GROUPS]
+        out_ref[:, group * WIDE : (group + 1) * WIDE] = dq_ref[...]
+        both = (own_ref[...].astype(F32) + got_ref[...].astype(F32)).astype(BF)
+        for pair in range(GROUP):
+            column = D + (group * GROUP + pair) * PAIR
+            start = 2 * pair * PAIR
+            out_ref[:, column : column + PAIR] = both[:, start : start + PAIR]
+            out_ref[:, column + D : column + D + PAIR] = both[:, start + PAIR : start + 2 * PAIR]
+
+
+def join(dqs, own, got):
+    rows = dqs[0].shape[0]
+    step = rows // 4
+    narrow = pl.BlockSpec((step, WIDE), lambda r: (r, 0))
+    double = pl.BlockSpec((step, 2 * WIDE), lambda r: (r, 0))
+    return pl.pallas_call(
+        join_kernel,
+        grid=(rows // step,),
+        in_specs=[narrow] * GROUPS + [double] * (2 * GROUPS),
+        out_specs=pl.BlockSpec((step, 3 * D), lambda r: (r, 0)),
+        out_shape=jax.ShapeDtypeStruct((rows, 3 * D), BF),
+        compiler_params=pltpu.CompilerParams(vmem_limit_bytes=LIMIT),
+    )(*dqs, *own, *got)
+
+
 def after(value, earlier):
     return lax.optimization_barrier((value, earlier))[0]
 
@@ -323,18 +363,17 @@
     queries = project(
         act_one, packed, cos_here, sin_here, 0, 1, GROUPS, GROUPS, HEAD_DIM**-0.5
     )
-    partial, both = [], []
+    partial, lse_parts, ctx = [], [], None
     last_done = queries
     for group in range(GROUPS):
         partial.append(forward(group, after(queries, last_done), kv_here[group], None))
         last_done = partial[group][1]
     for group in range(GROUPS):
-        both.append(
-            forward(group, after(queries, last_done), kv_there[group], partial[group])
+        ctx, lse = forward(
+            group, after(queries, last_done), kv_there[group], partial[group], ctx
         )
-        last_done = both[group][1]
-    ctx_parts, lse_parts = [pair[0] for pair in both], [pair[1] for pair in both]
-    ctx = jnp.concatenate(ctx_parts, axis=1)
+        lse_parts.append(lse)
+        last_done = lse
 
     attended = jnp.dot(ctx, full_out, preferred_element_type=F32)
     hidden = inputs + attended
@@ -363,26 +402,24 @@
     last_done = grad_ctx
     for group in range(GROUPS):
         dq_part, dkv_far = backward(
-            group, after(queries, last_done), kv_there[group], grad_ctx, ctx_parts[group], lse_parts[group],
+            group, after(queries, last_done), kv_there[group], grad_ctx, ctx, lse_parts[group],
             cos_there, sin_there, None,
         )
         dq_parts.append(dq_part)
         last_done = dq_part
         dkv_got.append(lax.ppermute(dkv_far, "seq", swap))
-    dqs, dks, dvs = [], [], []
-    for group in range(GROUPS):
-        last_done = (last_done, dkv_got[group] if group + 1 < GROUPS else joined)
+    dqs, dkvs = [], []
+    for group in range(GROUPS):
+        if group:
+            last_done = (last_done, dkv_got[group - 1])
         dq, dkv = backward(
-            group, after(queries, last_done), kv_here[group], grad_ctx, ctx_parts[group], lse_parts[group],
+            group, after(queries, last_done), kv_here[group], grad_ctx, ctx, lse_parts[group],
             cos_here, sin_here, dq_parts[group],
         )
         last_done = dq
-        dkv = (dkv.astype(F32) + dkv_got[group].astype(F32)).astype(BF)
         dqs.append(dq)
-        for start in range(0, 2 * WIDE, 2 * PAIR):
-            dks.append(dkv[:, start : start + PAIR])
-            dvs.append(dkv[:, start + PAIR : start + 2 * PAIR])
-    grad_proj = jnp.concatenate(dqs + dks + dvs, axis=1)
+        dkvs.append(dkv)
+    grad_proj = join(dqs, dkvs, dkv_got)
 
     grad_w_qkv = dot(act_one, grad_proj, 0, 0)
     full_qkv = packed[:, : 3 * D]

time: 442 us -> 418 us (0.946)
  local copies, waits for them, and re-layouts: 35.4 us -> 16.9 us
  waiting for transfers between devices: 92.3 us -> 104 us
  Pallas kernels: 189 us -> 182 us
    unnamed x94 -> x68, local copies, waits for them, and re-layouts: 26.4 us -> 10.7 us
    ppermute x3 -> x2, waiting for transfers between devices: 0.01 us -> 8.17 us  [body(): kv_there.append(lax.ppermute(kv, 'seq', swap))]
    pallas_call x6 -> x4, Pallas kernels: 100 us -> 93.7 us  [backward(): pl.pallas_call(functools.partial(backward_kernel, last, 256), grid=(GROUP...]
    ppermute x2, waiting for transfers between devices: 4.13 us -> 10.4 us  [owned(): other = lax.ppermute(part, 'seq', swap)]
    pallas_call x0 -> x1, Pallas kernels: none -> 6.12 us  [join(): pl.pallas_call(join_kernel, grid=(rows // step,), in_specs=[narrow] * GRO...]
    pallas_call x6 -> x4, Pallas kernels: 68.3 us -> 63.3 us  [forward(): pl.pallas_call(functools.partial(forward_kernel, last, 256), grid=(GROUP,...]
    dot_general x8, matrix products: 51.3 us -> 46.4 us  [dot(): lax.dot_general(a, b, (((a_dim,), (b_dim,)), ((), ())), preferred_element...]
    pallas_call x4 -> x3, Pallas kernels: 20.6 us -> 19.1 us  [project(): pl.pallas_call(functools.partial(project_kernel, turned, factor), grid=(c...]
  transfers between devices with their start and end apart: 13 -> 11, of which waited for: 3 -> 5; matrix products, arithmetic and copies ran while one was open for 14% -> 13% of each run, Pallas kernels for 43% -> 44%
where the time goes in v3:
time: 418 us; the launch traced here: 412 us
  Pallas kernels  182 us (44%)
  waiting for transfers between devices  104 us (25%)
  matrix products  63.2 us (15%)
  other arithmetic  23.9 us (6%)
  local copies, waits for them, and re-layouts  16.9 us (4%)
  between operations  14.5 us (3%)
  starting transfers between devices  7.89 us (2%)
    pallas_call x4, Pallas kernels, backward(): pl.pallas_call(functools.partial(backward_kernel, last, 256), grid=(GROUP...  93.7 us
    pallas_call x4, Pallas kernels, forward(): pl.pallas_call(functools.partial(forward_kernel, last, 256), grid=(GROUP,...  63.3 us
    dot_general x8, matrix products, dot(): lax.dot_general(a, b, (((a_dim,), (b_dim,)), ((), ())), preferred_element...  46.4 us
    reduce_scatter x1, waiting for transfers between devices, body(): lax.psum_scatter(grad_w_qkv, 'dp', scatter_dimension=0, tiled=True)  43.7 us
    all_gather x1, waiting for transfers between devices, body(): packed = lax.all_gather(packed, 'dp', axis=0, tiled=True)  41.1 us
    pallas_call x3, Pallas kernels, project(): pl.pallas_call(functools.partial(project_kernel, turned, factor), grid=(c...  19.1 us
    unnamed x68, local copies, waits for them, and re-layouts  10.7 us
    ppermute x2, waiting for transfers between devices, owned(): other = lax.ppermute(part, 'seq', swap)  10.4 us
  transfers between devices with their start and end apart: 11, of which 5 were waited for; matrix products, arithmetic and copies ran while one was open for 13% of the time, Pallas kernels for 44%

profile of v3, /device:TPU:0, one launch (start us, length us, event | category | flops | bytes accessed | tf_op | source)
XLA Modules:
  0.0 412.3 jit_solution(11207026316146334172)
XLA Ops:
  12.4 5.1 %fusion.29 = (f32[1024,32]{1,0:T(8,128)}, f32[1024,32]{1,0:T(8,128)}, f32[1024,32]{1,0:T(8,128)}, f32[1024,32]{1,0:T(8,128)S(1)}, f32[1024,32]{1,0:T(8,128)S(1)}, /*index=5*/f32[1024,32]{1,0:T(8,128)S(1)}) fusion(f32[32]{0:T(128)S(1)} %multiply_power_fusion, f32[1024]{0:T(1024)S(1)} %add_convert_fusion.2, f32[1024]{0:T(1024)S(1)} %add_convert_fusion.3), kind=kLoop, calls=%fused_computation.75 | loop fusion | flops 131072 | bytes 794752 | tf_op jit(solution)/shard_map/neg | solution.py:51
  20.2 41.1 %all-gather.4.cloned.1.call-done.w_ref = bf16[768,2432]{1,0:T(8,128)(2,1)} async-done(((bf16[48,2432]{1,0:T(8,128)(2,1)}), bf16[768,2432]{1,0:T(8,128)(2,1)}) %all-gather.4.cloned.1.call-update) | async-done | bytes 3735568 | tf_op jit(solution)/shard_map/all_gather | solution.py:342
  64.9 6.1 %shard_map.144.refs_1_.refs_2_ = bf16[1024,768]{1,0:T(8,128)(2,1)} custom-call(bf16[1024,768]{1,0:T(8,128)(2,1)} %fusion.14.act_ref, bf16[768,2432]{1,0:T(8,128)(2,1)} %all-gather.4.cloned.1.call-done.w_ref, f32[1024,128]{1,0:T(8,128)} %get-tuple-element.97.cos_ref.refs_6_, f32[1024,128]{1,0:T(8,128)} %get-tuple-element.98.sin_ref.refs_7_), custom_call_target="tpu_custom_call" | custom-call | flops 100663296 | bytes 131072 | tf_op jit(solution)/shard_map/pallas_call | solution.py:87
  72.4 6.0 %shard_map.146.refs_1_.refs_2_ = bf16[1024,768]{1,0:T(8,128)(2,1)} custom-call(bf16[1024,768]{1,0:T(8,128)(2,1)} %fusion.14.act_ref, bf16[768,2432]{1,0:T(8,128)(2,1)} %all-gather.4.cloned.1.call-done.w_ref, f32[1024,128]{1,0:T(8,128)} %get-tuple-element.97.cos_ref.refs_6_, f32[1024,128]{1,0:T(8,128)} %get-tuple-element.98.sin_ref.refs_7_), custom_call_target="tpu_custom_call" | custom-call | flops 100663296 | bytes 131072 | tf_op jit(solution)/shard_map/pallas_call | solution.py:87
  79.3 7.1 %shard_map.143.refs_0_ = bf16[1024,768]{1,0:T(8,128)(2,1)} custom-call(bf16[1024,768]{1,0:T(8,128)(2,1)} %fusion.14.act_ref, bf16[768,2432]{1,0:T(8,128)(2,1)} %all-gather.4.cloned.1.call-done.w_ref, f32[1024,128]{1,0:T(8,128)} %get-tuple-element.97.cos_ref.refs_6_, f32[1024,128]{1,0:T(8,128)} %get-tuple-element.98.sin_ref.refs_7_), custom_call_target="tpu_custom_call" | custom-call | flops 100663296 | bytes 131072 | tf_op jit(solution)/shard_map/pallas_call | solution.py:87
  86.4 14.0 %shard_map.145 = (f32[1024,384]{1,0:T(8,128)}, f32[1024,384]{1,0:T(8,128)}, f32[1024,384]{1,0:T(8,128)}) custom-call(bf16[1024,768]{1,0:T(8,128)(2,1)} %shard_map.143.refs_0_, bf16[1024,768]{1,0:T(8,128)(2,1)} %shard_map.144.refs_1_.refs_2_, bf16[1024,768]{1,0:T(8,128)(2,1)} %shard_map.144.refs_1_.refs_2_), custom_call_target="tpu_custom_call" | custom-call | flops 268435456 | bytes 131072 | tf_op jit(solution)/shard_map/pallas_call | solution.py:175
  100.4 13.9 %shard_map.147 = (f32[1024,384]{1,0:T(8,128)}, f32[1024,384]{1,0:T(8,128)}, f32[1024,384]{1,0:T(8,128)}) custom-call(bf16[1024,768]{1,0:T(8,128)(2,1)} %shard_map.143.refs_0_, bf16[1024,768]{1,0:T(8,128)(2,1)} %shard_map.146.refs_1_.refs_2_, bf16[1024,768]{1,0:T(8,128)(2,1)} %shard_map.146.refs_1_.refs_2_), custom_call_target="tpu_custom_call" | custom-call | flops 268435456 | bytes 131072 | tf_op jit(solution)/shard_map/pallas_call | solution.py:175
  115.5 17.9 %shard_map.148 = (bf16[1024,768]{1,0:T(8,128)(2,1)}, f32[1024,384]{1,0:T(8,128)}) custom-call(bf16[1024,768]{1,0:T(8,128)(2,1)} %shard_map.143.refs_0_, bf16[1024,768]{1,0:T(8,128)(2,1)} %copy-done.2, bf16[1024,768]{1,0:T(8,128)(2,1)} %copy-done.2, f32[1024,384]{1,0:T(8,128)} %get-tuple-element.40.refs_3_, f32[1024,384]{1,0:T(8,128)} %get-tuple-element.36.refs_4_, ...), custom_call_target="tpu_custom_call" | custom-call | flops 268435456 | bytes 131072 | tf_op jit(solution)/shard_map/pallas_call | solution.py:175
  133.4 8.2 %collective-permute-done.1.refs_1_.refs_2_ = bf16[1024,768]{1,0:T(8,128)(2,1)} collective-permute-done((bf16[1024,768]{1,0:T(8,128)(2,1)}, bf16[1024,768]{1,0:T(8,128)(2,1)}, u32[]{:S(2)}, u32[]{:S(2)}) %collective-permute-start.1) | collective-permute-done | bytes 1572896 | tf_op jit(solution)/shard_map/ppermute | solution.py:362
  141.5 17.5 %shard_map.149 = (bf16[1024,768]{1,0:T(8,128)(2,1)}, f32[1024,384]{1,0:T(8,128)}) custom-call(bf16[1024,768]{1,0:T(8,128)(2,1)} %shard_map.143.refs_0_, bf16[1024,768]{1,0:T(8,128)(2,1)} %collective-permute-done.1.refs_1_.refs_2_, bf16[1024,768]{1,0:T(8,128)(2,1)} %collective-permute-done.1.refs_1_.refs_2_, ...), custom_call_target="tpu_custom_call", output_to_operand_aliasing={{0}: (6, {})} | custom-call | flops 268435456 | bytes 131072 | tf_op jit(solution)/shard_map/pallas_call | solution.py:175
  164.2 6.8 %fusion.22 = f32[1024,2304]{1,0:T(8,128)} fusion(bf16[768,3072]{1,0:T(8,128)(2,1)S(1)} %bitcast.29, f32[1024,768]{1,0:T(8,128)S(1)} %get-tuple-element.93, f32[768]{0:T(1024)S(1)} %get-tuple-element.62, f32[1024]{0:T(1024)S(1)} %add_rsqrt_fusion, f32[1024]{0:T(1024)S(1)} %broadcast_multiply_fusion.4), kind=kOutput, calls=%fused_computation.47 | convolution fusion | flops 3627024384 | bytes 16134144 | tf_op jit(solution)/shard_map/dot_general | solution.py:382
  171.0 15.2 %add_convert_fusion = (bf16[1024,1152]{1,0:T(8,128)(2,1)S(1)}, f32[1024,1152]{1,0:T(8,128)S(1)}, f32[1024,1152]{1,0:T(8,128)S(1)}) fusion(f32[1024,2304]{1,0:T(8,128)} %fusion.22, bf16[1024,768]{1,0:T(8,128)(2,1)S(1)} %copy-done.14, bf16[1152,768]{1,0:T(8,128)(2,1)} %all-gather.8.cloned.1.call-done), kind=kOutput, calls=%fused_computation.9 | convolution fusion | flops 1898053632 | bytes 24576000 | tf_op jit(solution)/shard_map/dot_general | solution.py:66
  190.4 4.2 %convolution_convert_fusion = bf16[768,2304]{1,0:T(8,128)(2,1)S(1)} fusion(bf16[1024,1152]{1,0:T(8,128)(2,1)S(1)} %get-tuple-element.74, bf16[1024,1152]{1,0:T(8,128)(2,1)S(1)} %get-tuple-element.72, f32[1024,768]{1,0:T(8,128)S(1)} %copy-done.6, f32[768]{0:T(1024)S(1)} %get-tuple-element.62, f32[1024]{0:T(1024)S(1)} %add_rsqrt_fusion, ...), kind=kOutput, calls=%fused_computation.1 | convolution fusion | flops 3638231040 | bytes 11414528 | tf_op jit(solution)/shard_map/dot_general | solution.py:66
  194.6 6.2 %multiply_reduce_fusion.3 = (f32[1024]{0:T(1024)S(1)}, f32[1024]{0:T(1024)S(1)}, f32[1024,768]{1,0:T(8,128)S(1)}) fusion(f32[768]{0:T(1024)S(1)} %get-tuple-element.62, f32[1024]{0:T(1024)S(1)} %add_rsqrt_fusion, f32[1024,768]{1,0:T(8,128)S(1)} %copy-done.6, f32[1024]{0:T(1024)S(1)} %broadcast_multiply_fusion.4, ...), kind=kOutput, calls=%fused_computation.51 | convolution fusion | flops 3638032384 | bytes 14568448 | tf_op jit(solution)/shard_map/dot_general | solution.py:66
  213.4 5.1 %convolution_convert_fusion.3.refs_3_ = bf16[1024,768]{1,0:T(8,128)(2,1)} fusion(bf16[768,3072]{1,0:T(8,128)(2,1)} %all-gather.6.cloned.1.call-done, f32[1024,768]{1,0:T(8,128)} %copy-done.7), kind=kOutput, calls=%fused_computation.52 | convolution fusion | flops 1209532416 | bytes 5898240 | tf_op jit(solution)/shard_map/dot_general | solution.py:66
  218.5 23.0 %shard_map.150 = (f32[1024,384]{1,0:T(8,128)}, bf16[1024,768]{1,0:T(8,128)(2,1)}) custom-call(bf16[1024,768]{1,0:T(8,128)(2,1)} %shard_map.143.refs_0_, bf16[1024,768]{1,0:T(8,128)(2,1)} %copy-done.2, bf16[1024,768]{1,0:T(8,128)(2,1)} %copy-done.2, bf16[1024,768]{1,0:T(8,128)(2,1)} %convolution_convert_fusion.3.refs_3_, ...), custom_call_target="tpu_custom_call" | custom-call | flops 671088640 | bytes 131072 | tf_op jit(solution)/shard_map/pallas_call | solution.py:269
  243.1 23.2 %shard_map.151 = (f32[1024,384]{1,0:T(8,128)}, bf16[1024,768]{1,0:T(8,128)(2,1)}) custom-call(bf16[1024,768]{1,0:T(8,128)(2,1)} %shard_map.143.refs_0_, bf16[1024,768]{1,0:T(8,128)(2,1)} %collective-permute-done.1.refs_1_.refs_2_, bf16[1024,768]{1,0:T(8,128)(2,1)} %collective-permute-done.1.refs_1_.refs_2_, ...), custom_call_target="tpu_custom_call" | custom-call | flops 671088640 | bytes 131072 | tf_op jit(solution)/shard_map/pallas_call | solution.py:269
  266.7 23.6 %shard_map.152 = (bf16[1024,384]{1,0:T(8,128)(2,1)}, bf16[1024,768]{1,0:T(8,128)(2,1)}) custom-call(bf16[1024,768]{1,0:T(8,128)(2,1)} %shard_map.143.refs_0_, bf16[1024,768]{1,0:T(8,128)(2,1)} %shard_map.144.refs_1_.refs_2_, bf16[1024,768]{1,0:T(8,128)(2,1)} %shard_map.144.refs_1_.refs_2_, bf16[1024,768]{1,0:T(8,128)(2,1)} %convolution_convert_fusion.3.refs_3_, ...), custom_call_target="tpu_custom_call" | custom-call | flops 671088640 | bytes 131072 | tf_op jit(solution)/shard_map/pallas_call | solution.py:269
  290.4 23.9 %shard_map.153 = (bf16[1024,384]{1,0:T(8,128)(2,1)}, bf16[1024,768]{1,0:T(8,128)(2,1)}) custom-call(bf16[1024,768]{1,0:T(8,128)(2,1)} %shard_map.143.refs_0_, bf16[1024,768]{1,0:T(8,128)(2,1)} %shard_map.146.refs_1_.refs_2_, bf16[1024,768]{1,0:T(8,128)(2,1)} %shard_map.146.refs_1_.refs_2_, bf16[1024,768]{1,0:T(8,128)(2,1)} %convolution_convert_fusion.3.refs_3_, ...), custom_call_target="tpu_custom_call" | custom-call | flops 671088640 | bytes 131072 | tf_op jit(solution)/shard_map/pallas_call | solution.py:269
  315.4 6.1 %shard_map.154 = bf16[1024,2304]{1,0:T(8,128)(2,1)} custom-call(bf16[1024,384]{1,0:T(8,128)(2,1)} %get-tuple-element.54.refs_0_, bf16[1024,384]{1,0:T(8,128)(2,1)} %get-tuple-element.57.refs_1_, bf16[1024,768]{1,0:T(8,128)(2,1)} %get-tuple-element.58.refs_2_, bf16[1024,768]{1,0:T(8,128)(2,1)} %get-tuple-element.59.refs_3_, bf16[1024,768]{1,0:T(8,128)(2,1)} %copy-done.15, ...), custom_call_target="tpu_custom_call" | custom-call | tf_op jit(solution)/shard_map/pallas_call | solution.py:306
  321.5 7.9 %convolution_convert_fusion.1 = bf16[768,2304]{1,0:T(8,128)(2,1)} fusion(bf16[1024,768]{1,0:T(8,128)(2,1)S(1)} %copy-done.4, bf16[1024,2304]{1,0:T(8,128)(2,1)} %shard_map.154), kind=kOutput, calls=%fused_computation.2 | convolution fusion | flops 3625648128 | bytes 9830400 | tf_op jit(solution)/shard_map/dot_general | solution.py:66
  329.6 6.6 %add_convert_fusion.1 = bf16[1024,768]{1,0:T(8,128)(2,1)} fusion(f32[1024,768]{1,0:T(8,128)} %copy-done.5, bf16[1024,1152]{1,0:T(8,128)(2,1)} %copy-done.10, bf16[1152,768]{1,0:T(8,128)(2,1)} %all-gather.8.cloned.1.call-done), kind=kOutput, calls=%fused_computation.42 | convolution fusion | flops 1813512192 | bytes 8847360 | tf_op jit(solution)/shard_map/dot_general | solution.py:385
  344.6 6.2 %collective-permute-done.5 = bf16[264,768]{1,0:T(8,128)(2,1)S(1)} collective-permute-done((bf16[264,768]{1,0:T(8,128)(2,1)S(1)}, bf16[264,768]{1,0:T(8,128)(2,1)S(1)}, u32[]{:S(2)}, u32[]{:S(2)}) %collective-permute-start.5) | collective-permute-done | bytes 405536 | tf_op jit(solution)/shard_map/ppermute | solution.py:430
  353.2 43.7 %reduce-scatter.5.cloned.1.call-done = bf16[48,2304]{1,0:T(8,128)(2,1)} async-done(((bf16[768,2304]{1,0:T(8,128)(2,1)}), bf16[48,2304]{1,0:T(8,128)(2,1)}) %reduce-scatter.5.cloned.1.call-update) | async-done | bytes 221200 | tf_op jit(solution)/shard_map/reduce_scatter | solution.py:434
  (132 shorter events, 59.1 us)
Async XLA Ops:
  7.2 54.2 %all-gather.4.cloned.1.call-start = ((), (), s32[]{:S(2)}) async-start(), calls=%async_computation.2 | async-start | bytes 3969024 | tf_op jit(solution)/shard_map/all_gather | solution.py:342
  10.5 148.6 %all-gather.6.cloned.1.call-start = ((), (), s32[]{:S(2)}) async-start(), calls=%async_computation.3 | async-start | bytes 5013504 | tf_op jit(solution)/shard_map/all_gather | solution.py:343
  12.2 7.1 %copy-start.3 = (bf16[1024,768]{1,0:T(8,128)(2,1)S(1)}, bf16[1024,768]{1,0:T(8,128)(2,1)}, u32[]{:S(2)}) copy-start(bf16[1024,768]{1,0:T(8,128)(2,1)} %param.8) | copy-start | bytes 4718596
  12.3 158.7 %all-gather.8.cloned.1.call-start = ((), (), s32[]{:S(2)}) async-start(), calls=%async_computation.4 | async-start | bytes 1880064 | tf_op jit(solution)/shard_map/all_gather | solution.py:345
  19.6 45.3 %copy-start.20 = (f32[1024]{0:T(1024)}, f32[1024]{0:T(1024)S(1)}, u32[]{:S(2)}) copy-start(f32[1024]{0:T(1024)S(1)} %broadcast_multiply_fusion.5) | copy-start | bytes 12292
  20.2 44.7 %copy-start.24 = (f32[1024]{0:T(1024)}, f32[1024]{0:T(1024)S(1)}, u32[]{:S(2)}) copy-start(f32[1024]{0:T(1024)S(1)} %add_rsqrt_fusion.1) | copy-start | bytes 12292
  71.0 43.4 %collective-permute-start = (bf16[1024,768]{1,0:T(8,128)(2,1)}, bf16[1024,768]{1,0:T(8,128)(2,1)S(1)}, u32[]{:S(2)}, u32[]{:S(2)}) collective-permute-start(bf16[1024,768]{1,0:T(8,128)(2,1)} %shard_map.144.refs_1_.refs_2_), channel_id=1, source_target_pairs={{0,1},{1,0},{2,3},{3,2},{4,5},{5,4},{6,7},{7,6},{8,9},{9,8},{10,11... | collective-permute-start | bytes 4718600 | tf_op jit(solution)/shard_map/ppermute | solution.py:362
  78.4 63.1 %collective-permute-start.1 = (bf16[1024,768]{1,0:T(8,128)(2,1)}, bf16[1024,768]{1,0:T(8,128)(2,1)}, u32[]{:S(2)}, u32[]{:S(2)}) collective-permute-start(bf16[1024,768]{1,0:T(8,128)(2,1)} %shard_map.146.refs_1_.refs_2_), channel_id=1, source_target_pairs={{0,1},{1,0},{2,3},{3,2},{4,5},{5,4},{6,7},{7,6},{8,9},{9,8},{10,11... | collective-permute-start | bytes 4718600 | tf_op jit(solution)/shard_map/ppermute | solution.py:362
  79.1 250.4 %reduce-scatter.3.cloned.1.call-start = ((), (), s32[]{:S(2)}) async-start(), calls=%async_computation.5 | async-start | bytes 6893568 | tf_op jit(solution)/shard_map/reduce_scatter | solution.py:400
  164.2 6.8 %copy-start.14 = (bf16[1024,768]{1,0:T(8,128)(2,1)S(1)}, bf16[1024,768]{1,0:T(8,128)(2,1)}, u32[]{:S(2)}) copy-start(bf16[1024,768]{1,0:T(8,128)(2,1)} %param.15) | copy-start | bytes 4718596
  171.0 15.2 %copy-start.9 = (f32[1024,2304]{1,0:T(8,128)S(1)}, f32[1024,2304]{1,0:T(8,128)}, u32[]{:S(2)}) copy-start(f32[1024,2304]{1,0:T(8,128)} %fusion.22) | copy-start | bytes 28311556
  210.1 186.8 %reduce-scatter.5.cloned.1.call-start = ((), (), s32[]{:S(2)}) async-start(), calls=%async_computation.6 | async-start | bytes 3760128 | tf_op jit(solution)/shard_map/reduce_scatter | solution.py:434
  241.5 48.9 %collective-permute-start.2 = (bf16[1024,768]{1,0:T(8,128)(2,1)}, bf16[1024,768]{1,0:T(8,128)(2,1)S(1)}, u32[]{:S(2)}, u32[]{:S(2)}) collective-permute-start(bf16[1024,768]{1,0:T(8,128)(2,1)} %get-tuple-element.55), channel_id=1, source_target_pairs={{0,1},{1,0},{2,3},{3,2},{4,5},{5,4},{6,7},{7,6},{8,9},{9,8},{10,11... | collective-permute-start | bytes 4718600 | tf_op jit(solution)/shard_map/ppermute | solution.py:410
  266.3 48.0 %collective-permute-start.3 = (bf16[1024,768]{1,0:T(8,128)(2,1)}, bf16[1024,768]{1,0:T(8,128)(2,1)S(1)}, u32[]{:S(2)}, u32[]{:S(2)}) collective-permute-start(bf16[1024,768]{1,0:T(8,128)(2,1)} %get-tuple-element.60), channel_id=1, source_target_pairs={{0,1},{1,0},{2,3},{3,2},{4,5},{5,4},{6,7},{7,6},{8,9},{9,8},{10,11... | collective-permute-start | bytes 4718600 | tf_op jit(solution)/shard_map/ppermute | solution.py:410
  290.4 23.9 %copy-start.15 = (bf16[1024,768]{1,0:T(8,128)(2,1)}, bf16[1024,768]{1,0:T(8,128)(2,1)S(1)}, u32[]{:S(2)}) copy-start(bf16[1024,768]{1,0:T(8,128)(2,1)S(1)} %collective-permute-done.2.refs_4_) | copy-start | bytes 4718596
  329.5 6.7 %slice-start = ((s8[4718592]{0:T(1024)(128)(4,1)}), s8[524288]{0:T(1024)(128)(4,1)S(1)}, s32[]{:S(2)}) async-start(s8[4718592]{0:T(1024)(128)(4,1)} %bitcast.19), calls=%async_computation.7 | async-start | bytes 1048576
  329.5 6.7 %copy-start.1 = (bf16[768,2432]{1,0:T(8,128)(2,1)S(1)}, bf16[768,2432]{1,0:T(8,128)(2,1)}, u32[]{:S(2)}) copy-start(bf16[768,2432]{1,0:T(8,128)(2,1)} %all-gather.4.cloned.1.call-done.w_ref) | copy-start | bytes 11206660
  329.5 6.7 %slice-start.1 = ((s8[4718592]{0:T(1024)(128)(4,1)}), s8[4194304]{0:T(1024)(128)(4,1)S(1)}, s32[]{:S(2)}) async-start(s8[4718592]{0:T(1024)(128)(4,1)} %bitcast.19), calls=%async_computation.8 | async-start | bytes 8388608
  340.5 10.3 %collective-permute-start.5 = (bf16[264,768]{1,0:T(8,128)(2,1)S(1)}, bf16[264,768]{1,0:T(8,128)(2,1)S(1)}, u32[]{:S(2)}, u32[]{:S(2)}) collective-permute-start(bf16[264,768]{1,0:T(8,128)(2,1)S(1)} %copy-done.19), channel_id=1, source_target_pairs={{0,1},{1,0},{2,3},{3,2},{4,5},{5,4},{6,7},{7,6},{8,9},{9,8},{10,11... | collective-permute-start | bytes 1216520 | tf_op jit(solution)/shard_map/ppermute | solution.py:430
  344.5 7.7 %copy-start.17 = (bf16[48,2304]{1,0:T(8,128)(2,1)S(1)}, bf16[48,2304]{1,0:T(8,128)(2,1)}, u32[]{:S(2)}) copy-start(bf16[48,2304]{1,0:T(8,128)(2,1)} %param.13) | copy-start | bytes 663556
  344.5 53.8 %copy-start.26 = (bf16[48]{0:T(256)(128)(2,1)S(1)}, bf16[48]{0:T(256)(128)(2,1)}, u32[]{:S(2)}) copy-start(bf16[48]{0:T(256)(128)(2,1)} %param.12) | copy-start | bytes 292
  344.5 58.5 %copy-start.18 = (bf16[48,2304]{1,0:T(8,128)(2,1)S(1)}, bf16[48,2304]{1,0:T(8,128)(2,1)}, u32[]{:S(2)}) copy-start(bf16[48,2304]{1,0:T(8,128)(2,1)} %param.10) | copy-start | bytes 663556
  344.5 60.4 %copy-start.27 = (bf16[48]{0:T(256)(128)(2,1)S(1)}, bf16[48]{0:T(256)(128)(2,1)}, u32[]{:S(2)}) copy-start(bf16[48]{0:T(256)(128)(2,1)} %param.9) | copy-start | bytes 292
  396.9 6.1 %collective-permute-start.4 = (bf16[48,2304]{1,0:T(8,128)(2,1)}, bf16[48,2304]{1,0:T(8,128)(2,1)S(1)}, u32[]{:S(2)}, u32[]{:S(2)}) collective-permute-start(bf16[48,2304]{1,0:T(8,128)(2,1)} %reduce-scatter.5.cloned.1.call-done), channel_id=1, source_target_pairs={{0,1},{1,0},{2,3},{3,2},{4,5},{5,4},{6,7},{7,6},{8,9},{9,8},{10,11... | collective-permute-start | bytes 663560 | tf_op jit(solution)/shard_map/ppermute | solution.py:430
  (19 other events, 62.5 us)
Sparse Core Ops, SparseCore 0:
  10.7 50.5 all-gather.3
  64.2 52.4 all-gather.5
  118.8 38.9 all-gather.7
  210.2 86.2 reduce-scatter.2
  329.7 67.1 reduce-scatter.4
